TPU v7x, 256 devices: a whole 4x4x8 slice. The times are simulated.
256 devices in a mesh: gz: 8 (over y, core), xy: 32 (over z, x).
Axes of the slice: x: 4, y: 4, z: 8, core: 2. Of those that a mesh axis runs over, the one named last changes fastest.
Arguments:
- features: bfloat16 [2, 64, 128, 128, 128], P(None, None, 'gz', 'xy'), may hold values from -6 to 6
- cotangent: bfloat16 [2, 64, 128, 128, 128], P(None, None, 'gz', 'xy'), may hold values from -1.5 to 1.5
- spectral: bfloat16 [32, 32, 32, 64, 128], P('xy', 'gz'), may hold values from -0.75 to 0.75
- pointwise: bfloat16 [64, 64], replicated, may hold values from -0.75 to 0.75
- channel_bias: float32 [64], replicated, may hold values from -3 to 3
Outputs:
- layer_out: bfloat16 [2, 64, 128, 128, 128], P(None, None, 'gz', 'xy')
- input_grad: bfloat16 [2, 64, 128, 128, 128], P(None, None, 'gz', 'xy')
- spectral_grad: bfloat16 [32, 32, 32, 64, 128], P('xy', 'gz')
All inputs are finite; a program needn't handle non-finite values.
Results may differ from a plain program's by a relative error of at most 0.025.
Values may be sent and summed in bfloat16 or wider, within the bound.
No kernel may reach another device: no remote copies, remote signals or barrier semaphores. Data moves between devices by JAX's collectives and lax.ppermute only.
A program may use at most 128 MiB of HBM per device.

v0:
```python
import functools
import math

import jax
import jax.numpy as jnp
import ml_dtypes
import numpy as np
from jax import lax
from jax.experimental import pallas as pl
from jax.experimental.pallas import tpu as pltpu
from jax.sharding import PartitionSpec as P

C = 64
NX = 128
NY = 128
NZ = 128
MX = 32
MY = 32
MZ = 32
BATCH = 2
GZ = 8
XY = 32
BC = BATCH * C
ZL = NZ // GZ
XL = NX // XY
ZP = 2
PAIRS = ZL // ZP
ROWS = ZP * 2 * XL
BF = jnp.bfloat16
F32 = jnp.float32
FORWARD = (NX * NY * NZ) ** (-0.5)
INVERSE = 0.5 * (MX * MY * MZ) ** (-0.5)


def rounded(values):
    return values.astype(np.float32).astype(ml_dtypes.bfloat16).astype(np.float32)


def cos_sin(length, modes, folded):
    freq = np.arange(modes)
    if folded:
        freq = np.where(freq < modes // 2, freq, length - modes + freq)
    phase = (np.arange(length)[:, None] * freq[None, :]) % length
    angle = phase.astype(np.float32) * np.float32(2.0 * math.pi / length)
    return rounded(np.cos(angle)), rounded(np.sin(angle))


@functools.lru_cache(maxsize=None)
def tables():
    cy, sy = cos_sin(NY, MY, False)
    cx, sx = cos_sin(NX, MX, True)
    cz, sz = cos_sin(NZ, MZ, True)
    same = np.eye(ZP * XL, dtype=np.float32).reshape(ZP, XL, ZP, XL)
    part = np.stack([cy, -sy])
    unit = np.einsum("ryk,zxwv->kzrxwvy", part, same).reshape(MY * ROWS, ZP * XL * NY)
    scale = np.where(np.arange(MY) == 0, 1.0, 2.0).astype(np.float32)
    doubled = unit * np.repeat(scale, ROWS)[:, None]
    z2 = np.eye(ZP, dtype=np.float32)
    fx = np.stack([np.stack([cx, sx]), np.stack([-sx, cx])])
    fx = fx.reshape(2, 2, XY, XL, MX)
    x_fwd = np.einsum("sopvk,zw->kszpwov", fx, z2).reshape(MX * 2 * ZP, XY * ROWS)
    gx = np.stack([np.stack([cx, -sx]), np.stack([sx, cx])])
    gx = gx.reshape(2, 2, XY, XL, MX)
    x_inv = np.einsum("sopvk,zw->pzsvkow", gx, z2).reshape(XY * ROWS, MX * 2 * ZP)
    kx = MX // GZ
    kxe = np.eye(kx, dtype=np.float32)
    fz = np.stack([np.stack([cz, sz]), np.stack([-sz, cz])])
    fz = fz.reshape(2, 2, GZ, PAIRS, ZP, MZ)
    z_fwd = np.einsum("sogjzm,kl->skmgjloz", fz, kxe).reshape(2 * kx * MZ, GZ * PAIRS * kx * 2 * ZP)
    gz = np.stack([np.stack([cz, -sz]), np.stack([sz, cz])])
    gz = gz.reshape(2, 2, GZ, PAIRS, ZP, MZ)
    z_inv = np.einsum("sogjzm,kl->gjkszolm", gz, kxe).reshape(GZ * PAIRS * kx * 2 * ZP, 2 * kx * MZ)
    made = dict(
        unit=unit,
        doubled=doubled,
        doubled_t=doubled.T,
        x_fwd=x_fwd,
        x_inv=x_inv,
        z_fwd=z_fwd,
        z_inv=z_inv,
    )
    return {k: np.ascontiguousarray(v).astype(ml_dtypes.bfloat16) for k, v in made.items()}


def dot(a, b, dims=((1,), (0,))):
    return lax.dot_general(a, b, (dims, ((), ())), preferred_element_type=F32)


VM = 48 * 1024 * 1024


def call(kernel, outs, grid, in_specs, out_specs, scratch, name, flops, nbytes):
    return pl.pallas_call(
        kernel,
        out_shape=outs,
        grid=grid,
        in_specs=in_specs,
        out_specs=out_specs,
        scratch_shapes=scratch,
        name=name,
        compiler_params=pltpu.CompilerParams(vmem_limit_bytes=VM),
        cost_estimate=pl.CostEstimate(flops=flops, bytes_accessed=nbytes, transcendentals=0),
    )


STEPS = PAIRS // 2
CELLS = ZP * XL
STEP_CELLS = 2 * CELLS


def whole(shape):
    return pl.BlockSpec(shape, lambda i: (0,) * len(shape))


def first_kernel(x_ref, table_ref, out_ref, wide_ref):
    wide_ref[...] = x_ref[...].astype(F32).reshape(BC * STEP_CELLS, NY)
    rows = []
    for j in range(2):
        cells = [
            wide_ref[pl.ds(j * CELLS + t, BC, stride=STEP_CELLS), :].astype(BF)
            for t in range(CELLS)
        ]
        rows.append(jnp.concatenate(cells, axis=1))
    both = jnp.concatenate(rows, axis=0)
    modes = (dot(table_ref[...], both, ((1,), (1,))) * FORWARD).astype(BF)
    for j in range(2):
        out_ref[:, j * ROWS : (j + 1) * ROWS, :] = modes[:, j * BC : (j + 1) * BC].reshape(
            MY, ROWS, BC
        )


def y_first(x, table):
    return call(
        first_kernel,
        jax.ShapeDtypeStruct((MY, PAIRS * ROWS, BC), BF),
        (STEPS,),
        [
            pl.BlockSpec((BC, STEP_CELLS, NY), lambda i: (0, i, 0)),
            whole(table.shape),
        ],
        pl.BlockSpec((MY, 2 * ROWS, BC), lambda i: (0, i, 0)),
        [pltpu.VMEM((BC * STEP_CELLS, NY), F32)],
        "y_first",
        2 << 29,
        4 << 20,
    )(x, table)


def to_lanes_kernel(x_ref, out_ref, wide_ref):
    wide_ref[...] = x_ref[...].astype(F32).reshape(BC * STEP_CELLS, NY)
    for t in range(STEP_CELLS):
        cell = wide_ref[pl.ds(t, BC, stride=STEP_CELLS), :]
        out_ref[t * NY : (t + 1) * NY, :] = cell.T.astype(BF)


def to_lanes(x):
    return call(
        to_lanes_kernel,
        jax.ShapeDtypeStruct((ZL * XL * NY, BC), BF),
        (STEPS,),
        [pl.BlockSpec((BC, STEP_CELLS, NY), lambda i: (0, i, 0))],
        pl.BlockSpec((STEP_CELLS * NY, BC), lambda i: (i, 0)),
        [pltpu.VMEM((BC * STEP_CELLS, NY), F32)],
        "to_lanes",
        0,
        12 << 20,
    )(x)


def from_lanes_kernel(x_ref, out_ref, wide_ref):
    for t in range(STEP_CELLS):
        cell = x_ref[t * NY : (t + 1) * NY, :].astype(F32)
        wide_ref[pl.ds(t, BC, stride=STEP_CELLS), :] = cell.T
    out_ref[...] = wide_ref[...].reshape(BC, STEP_CELLS, NY).astype(BF)


def from_lanes(x):
    return call(
        from_lanes_kernel,
        jax.ShapeDtypeStruct((BC, ZL * XL, NY), BF),
        (STEPS,),
        [pl.BlockSpec((STEP_CELLS * NY, BC), lambda i: (i, 0))],
        pl.BlockSpec((BC, STEP_CELLS, NY), lambda i: (0, i, 0)),
        [pltpu.VMEM((BC * STEP_CELLS, NY), F32)],
        "from_lanes",
        0,
        12 << 20,
    )(x)


def x_forward_kernel(recv_ref, table_ref, out_ref):
    wide = jnp.concatenate(
        [
            recv_ref[:, j * ROWS : (j + 1) * ROWS, :].reshape(XY * ROWS, BC)
            for j in range(2)
        ],
        axis=1,
    )
    done = dot(table_ref[...], wide).astype(BF)
    for j in range(2):
        out_ref[:, j * ROWS : (j + 1) * ROWS, :] = done[:, j * BC : (j + 1) * BC].reshape(
            GZ, ROWS, BC
        )


def x_forward(recv, table):
    return call(
        x_forward_kernel,
        jax.ShapeDtypeStruct((GZ, PAIRS * ROWS, BC), BF),
        (STEPS,),
        [
            pl.BlockSpec((XY, 2 * ROWS, BC), lambda i: (0, i, 0)),
            whole(table.shape),
        ],
        pl.BlockSpec((GZ, 2 * ROWS, BC), lambda i: (0, i, 0)),
        [],
        "x_forward",
        1 << 27,
        2 << 20,
    )(recv, table)


def x_inverse_kernel(recv_ref, table_ref, out_ref):
    wide = jnp.concatenate(
        [
            recv_ref[:, j * ROWS : (j + 1) * ROWS, :].reshape(GZ * ROWS, BC)
            for j in range(2)
        ],
        axis=1,
    )
    done = dot(table_ref[...], wide).astype(BF)
    for j in range(2):
        out_ref[:, j * ROWS : (j + 1) * ROWS, :] = done[:, j * BC : (j + 1) * BC].reshape(
            XY, ROWS, BC
        )


def x_inverse(recv, table):
    return call(
        x_inverse_kernel,
        jax.ShapeDtypeStruct((XY, PAIRS * ROWS, BC), BF),
        (STEPS,),
        [
            pl.BlockSpec((GZ, 2 * ROWS, BC), lambda i: (0, i, 0)),
            whole(table.shape),
        ],
        pl.BlockSpec((XY, 2 * ROWS, BC), lambda i: (0, i, 0)),
        [],
        "x_inverse",
        1 << 27,
        2 << 20,
    )(recv, table)


PAIR_CELLS = CELLS * NY


def middle_kernel(
    recv_ref, x_ref, cot_ref, inv_ref, fwd_ref, mix_ref, bias_ref, send_ref, layer_ref, pre_ref, sum_ref, cat_ref
):
    wide = jnp.concatenate(
        [
            recv_ref[:, j * ROWS : (j + 1) * ROWS, :].reshape(MY * ROWS, BC)
            for j in range(2)
        ],
        axis=1,
    )
    sum_ref[...] = dot(inv_ref[...], wide)

    def chunk(step, _):
        at = pl.ds(pl.multiple_of(step * NY, NY), NY)
        for j in range(2):
            rows = pl.ds(pl.multiple_of(j * PAIR_CELLS + step * NY, NY), NY)
            local = dot(x_ref[rows, :], mix_ref[...])
            p = sum_ref[at, j * BC : (j + 1) * BC] * INVERSE + local + bias_ref[...]
            square = p * p
            inner = 0.7978845608 + (0.7978845608 * 0.044715) * square
            half = 0.5 + 0.5 * jnp.tanh(p * inner)
            layer_ref[rows, :] = (p * half).astype(BF)
            tail = (2.0 * 0.7978845608) + (6.0 * 0.7978845608 * 0.044715) * square
            slope = half + half * (1.0 - half) * (p * tail)
            grad = (cot_ref[rows, :].astype(F32) * slope).astype(BF)
            pre_ref[rows, :] = grad
            cat_ref[at, j * BC : (j + 1) * BC] = grad
        return 0

    lax.fori_loop(0, CELLS, chunk, 0)
    modes = (dot(fwd_ref[...], cat_ref[...]) * INVERSE).astype(BF)
    for j in range(2):
        send_ref[:, j * ROWS : (j + 1) * ROWS, :] = modes[:, j * BC : (j + 1) * BC].reshape(
            MY, ROWS, BC
        )


def middle(recv, x, cot, inv, fwd, mix, bias):
    flat = jax.ShapeDtypeStruct((ZL * XL * NY, BC), BF)
    step_rows = pl.BlockSpec((STEP_CELLS * NY, BC), lambda i: (i, 0))
    block = pl.BlockSpec((MY, 2 * ROWS, BC), lambda i: (0, i, 0))
    return call(
        middle_kernel,
        [jax.ShapeDtypeStruct((MY, PAIRS * ROWS, BC), BF), flat, flat],
        (STEPS,),
        [
            block,
            step_rows,
            step_rows,
            whole(inv.shape),
            whole(fwd.shape),
            whole(mix.shape),
            whole(bias.shape),
        ],
        [block, step_rows, step_rows],
        [
            pltpu.VMEM((PAIR_CELLS, 2 * BC), F32),
            pltpu.VMEM((PAIR_CELLS, 2 * BC), BF),
        ],
        "middle",
        4 << 29,
        12 << 20,
    )(recv, x, cot, inv, fwd, mix, bias)


def last_kernel(recv_ref, pre_ref, inv_ref, mix_ref, out_ref, wide_ref):
    for j in range(2):
        modes = recv_ref[:, j * ROWS : (j + 1) * ROWS, :].reshape(MY * ROWS, BC)
        cells = dot(modes, inv_ref[...], ((0,), (0,))) * FORWARD
        cells += dot(mix_ref[...], pre_ref[j * PAIR_CELLS : (j + 1) * PAIR_CELLS, :], ((1,), (1,)))
        for t in range(CELLS):
            wide_ref[pl.ds(j * CELLS + t, BC, stride=STEP_CELLS), :] = cells[:, t * NY : (t + 1) * NY]
    out_ref[...] = wide_ref[...].reshape(BC, STEP_CELLS, NY).astype(BF)


def last(recv, pre, inv, mix):
    return call(
        last_kernel,
        jax.ShapeDtypeStruct((BC, ZL * XL, NY), BF),
        (STEPS,),
        [
            pl.BlockSpec((MY, 2 * ROWS, BC), lambda i: (0, i, 0)),
            pl.BlockSpec((STEP_CELLS * NY, BC), lambda i: (i, 0)),
            whole(inv.shape),
            whole(mix.shape),
        ],
        pl.BlockSpec((BC, STEP_CELLS, NY), lambda i: (0, i, 0)),
        [pltpu.VMEM((BC * STEP_CELLS, NY), F32)],
        "last",
        4 << 29,
        8 << 20,
    )(recv, pre, inv, mix)


def exchange(x, axis):
    return lax.all_to_all(x, axis, split_axis=0, concat_axis=0, tiled=True)


KX = MX // GZ


def z_forward(recv, table):
    modes = dot(table, recv.reshape(GZ * PAIRS * ROWS, BC))
    return modes.astype(BF).reshape(2, KX, MZ, BATCH, C)


def z_inverse(modes, table):
    return dot(table, modes.reshape(2 * KX * MZ, BC)).astype(BF).reshape(GZ, PAIRS * ROWS, BC)


def body(features, cotangent, spectral, pointwise, channel_bias):
    t = {k: jnp.asarray(v) for k, v in tables().items()}
    x = features.reshape(BC, ZL * XL, NY)
    cot = cotangent.reshape(BC, ZL * XL, NY)
    weights = spectral[0]
    mix = jnp.zeros((BATCH, C, BATCH, C), BF)
    mix = mix.at[0, :, 0, :].set(pointwise).at[1, :, 1, :].set(pointwise).reshape(BC, BC)
    bias = jnp.tile(channel_bias, BATCH)[None, :]

    recv = exchange(y_first(x, t["unit"]), "xy")
    x_lanes = to_lanes(x)
    recv = exchange(x_forward(recv, t["x_fwd"]), "gz")
    spectra = z_forward(recv, t["z_fwd"])
    products = jnp.einsum("rkmbi,kmio->rkmbo", spectra, weights, preferred_element_type=F32)
    mixed = jnp.stack(
        [
            products[0, ..., :C] - products[1, ..., C:],
            products[0, ..., C:] + products[1, ..., :C],
        ]
    ).astype(BF)
    recv = exchange(z_inverse(mixed, t["z_inv"]), "gz")
    recv = exchange(x_inverse(recv, t["x_inv"]), "xy")
    cot_lanes = to_lanes(cot)
    send, layer, pre = middle(
        recv, x_lanes, cot_lanes, t["doubled_t"], t["doubled"], mix, bias
    )
    recv = exchange(send, "xy")
    layer_out = from_lanes(layer)
    recv = exchange(x_forward(recv, t["x_fwd"]), "gz")
    mode_grad = z_forward(recv, t["z_fwd"])
    real, imag = mode_grad[0], mode_grad[1]
    paired = jnp.stack(
        [
            jnp.concatenate([real, imag], axis=-1),
            jnp.concatenate([imag, -real], axis=-1),
        ]
    )
    spectra_grad = jnp.einsum(
        "rkmbo,kmio->rkmbi", paired, weights, preferred_element_type=F32
    ).astype(BF)
    recv = exchange(z_inverse(spectra_grad, t["z_inv"]), "gz")
    recv = exchange(x_inverse(recv, t["x_inv"]), "xy")
    spectral_grad = jnp.einsum(
        "rkmbi,rkmbo->kmio", spectra, paired, preferred_element_type=F32
    ).astype(BF)
    input_grad = last(recv, pre, t["unit"], mix)
    return (
        layer_out.reshape(features.shape),
        input_grad.reshape(features.shape),
        spectral_grad[None],
    )


def solution(mesh):
    field = P(None, None, "gz", "xy", None)
    modes = P("xy", "gz", None, None, None)
    return jax.shard_map(
        body,
        mesh=mesh,
        in_specs=(field, field, modes, P(), P()),
        out_specs=(field, field, modes),
        check_vma=False,
    )
```

profile of v0, /device:TPU:2, one launch (start us, length us, event | category | flops | bytes accessed | tf_op | source)
XLA Modules:
  0.0 222.1 jit_solution(9370325546207778966)
XLA Ops:
  0.7 1.7 copy-done.1
  2.4 1.2 copy-done.7
  3.6 2.9 %y_first.1 = bf16[32,128,128]{2,1,0:T(8,128)(2,1)S(1)} custom-call(bf16[128,64,128]{2,1,0:T(8,128)(2,1)S(1)} %bitcast.56, bf16[512,1024]{1,0:T(8,128)(2,1)S(1)} %copy-done.7), custom_call_target="tpu_custom_call" | custom-call | flops 1073741824 | bytes 4194304 | tf_op jit(solution)/shard_map/y_first/pallas_call | solution.py:133
  6.6 39.6 %all_to_all.40.recv_ref = bf16[32,128,128]{2,1,0:T(8,128)(2,1)S(1)} all-to-all(bf16[32,128,128]{2,1,0:T(8,128)(2,1)S(1)} %y_first.1), channel_id=1, replica_groups=mesh['gz'=8,'xy'=32] {'xy'}, dimensions={0} | all-to-all | bytes 2097152 | tf_op jit(solution)/shard_map/all_to_all | solution.py:353
  46.2 0.9 x_forward.2
  47.1 11.8 %all_to_all.41 = bf16[8,128,128]{2,1,0:T(8,128)(2,1)S(1)} all-to-all(bf16[8,128,128]{2,1,0:T(8,128)(2,1)S(1)} %x_forward.2), channel_id=1, replica_groups=mesh['gz'=8,'xy'=32] {'gz'}, dimensions={0} | all-to-all | bytes 524288 | tf_op jit(solution)/shard_map/all_to_all | solution.py:353
  58.9 0.3 fusion.16
  59.3 0.1 copy.25
  59.5 0.7 fusion.7
  60.2 0.3 fusion.19
  60.5 0.2 pad_maximum_fusion
  60.9 0.1 convert_element_type.40
  61.0 0.3 fusion.5
  61.3 0.2 copy.28
  61.5 9.9 %all_to_all.42.recv_ref = bf16[8,128,128]{2,1,0:T(8,128)(2,1)S(1)} all-to-all(bf16[8,128,128]{2,1,0:T(8,128)(2,1)S(1)} %bitcast.63), channel_id=1, replica_groups=mesh['gz'=8,'xy'=32] {'gz'}, dimensions={0} | all-to-all | bytes 524288 | tf_op jit(solution)/shard_map/all_to_all | solution.py:353
  71.4 2.1 x_inverse.2
  73.5 5.6 %all-to-all-start.3 = ((bf16[32,128,128]{2,1,0:T(8,128)(2,1)}), bf16[32,128,128]{2,1,0:T(8,128)(2,1)S(1)}, u32[]{:S(2)}, u32[]{:S(2)}) async-start(bf16[32,128,128]{2,1,0:T(8,128)(2,1)} %x_inverse.2), calls=%async_computation.3 | async-start | bytes 2097152 | tf_op jit(solution)/shard_map/all_to_all | solution.py:353
  79.1 1.6 copy-done.2
  80.7 2.0 to_lanes.2.x_ref
  82.7 1.3 copy-done.5
  84.3 1.6 copy-done.3
  85.9 2.0 to_lanes.3.cot_ref
  87.9 1.3 copy-done.6
  89.2 17.6 %all-to-all-done.3.recv_ref = bf16[32,128,128]{2,1,0:T(8,128)(2,1)S(1)} async-done(((bf16[32,128,128]{2,1,0:T(8,128)(2,1)}), bf16[32,128,128]{2,1,0:T(8,128)(2,1)S(1)}, u32[]{:S(2)}, u32[]{:S(2)}) %all-to-all-start.3) | async-done | bytes 1048608 | tf_op jit(solution)/shard_map/all_to_all | solution.py:353
  106.8 1.2 copy-done.11
  108.0 1.2 copy-done.12
  109.3 13.4 %middle.1 = (bf16[32,128,128]{2,1,0:T(8,128)(2,1)S(1)}, bf16[8192,128]{1,0:T(8,128)(2,1)}, bf16[8192,128]{1,0:T(8,128)(2,1)}) custom-call(bf16[32,128,128]{2,1,0:T(8,128)(2,1)S(1)} %all-to-all-done.3.recv_ref, bf16[8192,128]{1,0:T(8,128)(2,1)} %copy-done.5, bf16[8192,128]{1,0:T(8,128)(2,1)} %copy-done.6, bf16[1024,512]{1,0:T(8,128)(2,1)S(1)} %copy-done.11, ...), custom_call_target="tpu_custom_call" | custom-call | flops 2147483648 | bytes 12582912 | tf_op jit(solution)/shard_map/middle/pallas_call | solution.py:299
  122.6 32.2 %all_to_all.43.recv_ref = bf16[32,128,128]{2,1,0:T(8,128)(2,1)S(1)} all-to-all(bf16[32,128,128]{2,1,0:T(8,128)(2,1)S(1)} %get-tuple-element.31), channel_id=1, replica_groups=mesh['gz'=8,'xy'=32] {'xy'}, dimensions={0} | all-to-all | bytes 2097152 | tf_op jit(solution)/shard_map/all_to_all | solution.py:353
  154.8 0.9 x_forward.3
  155.8 10.0 %all_to_all.44 = bf16[8,128,128]{2,1,0:T(8,128)(2,1)S(1)} all-to-all(bf16[8,128,128]{2,1,0:T(8,128)(2,1)S(1)} %x_forward.3), channel_id=1, replica_groups=mesh['gz'=8,'xy'=32] {'gz'}, dimensions={0} | all-to-all | bytes 524288 | tf_op jit(solution)/shard_map/all_to_all | solution.py:353
  165.8 0.3 fusion.17
  166.1 0.1 copy.31
  166.6 0.4 maximum_bitcast_fusion
  167.0 0.6 copy-done.20
  167.6 1.2 fusion.13
  169.1 0.3 fusion.6
  169.4 0.2 copy.33
  169.5 9.9 %all_to_all.45.recv_ref = bf16[8,128,128]{2,1,0:T(8,128)(2,1)S(1)} all-to-all(bf16[8,128,128]{2,1,0:T(8,128)(2,1)S(1)} %bitcast.64), channel_id=1, replica_groups=mesh['gz'=8,'xy'=32] {'gz'}, dimensions={0} | all-to-all | bytes 524288 | tf_op jit(solution)/shard_map/all_to_all | solution.py:353
  179.5 2.1 x_inverse.3
  181.6 5.6 %all-to-all-start.7 = ((bf16[32,128,128]{2,1,0:T(8,128)(2,1)}), bf16[32,128,128]{2,1,0:T(8,128)(2,1)S(1)}, u32[]{:S(2)}, u32[]{:S(2)}) async-start(bf16[32,128,128]{2,1,0:T(8,128)(2,1)} %x_inverse.3), calls=%async_computation.7 | async-start | bytes 2097152 | tf_op jit(solution)/shard_map/all_to_all | solution.py:353
  187.2 1.6 copy-done.4
  188.8 2.8 %from_lanes.1 = bf16[128,64,128]{2,1,0:T(8,128)(2,1)} custom-call(bf16[8192,128]{1,0:T(8,128)(2,1)S(1)} %copy-done.4), custom_call_target="tpu_custom_call" | custom-call | bytes 12582912 | tf_op jit(solution)/shard_map/from_lanes/pallas_call | solution.py:178
  191.5 0.9 fusion.20
  192.4 1.5 copy.51
  193.9 20.9 %all-to-all-done.7.recv_ref = bf16[32,128,128]{2,1,0:T(8,128)(2,1)S(1)} async-done(((bf16[32,128,128]{2,1,0:T(8,128)(2,1)}), bf16[32,128,128]{2,1,0:T(8,128)(2,1)S(1)}, u32[]{:S(2)}, u32[]{:S(2)}) %all-to-all-start.7) | async-done | bytes 1048608 | tf_op jit(solution)/shard_map/all_to_all | solution.py:353
  214.8 1.2 copy-done.8
  216.1 1.6 copy-done.13
  217.7 4.5 %last.1 = bf16[128,64,128]{2,1,0:T(8,128)(2,1)} custom-call(bf16[32,128,128]{2,1,0:T(8,128)(2,1)S(1)} %all-to-all-done.7.recv_ref, bf16[8192,128]{1,0:T(8,128)(2,1)S(1)} %copy-done.13, bf16[512,1024]{1,0:T(8,128)(2,1)S(1)} %copy-done.8, bf16[128,128]{1,0:T(8,128)(2,1)S(1)} %reshape.127.mix_ref), custom_call_target="tpu_custom_call" | custom-call | flops 2147483648 | bytes 8388608 | tf_op jit(solution)/shard_map/last/pallas_call | solution.py:334
  (51 shorter events, 1.2 us)
Async XLA Ops:
  0.6 58.9 %copy-start = (bf16[1,4,32,64,128]{4,3,2,1,0:T(8,128)(2,1)S(1)}, bf16[1,4,32,64,128]{4,3,2,1,0:T(8,128)(2,1)}, u32[]{:S(2)}) copy-start(bf16[1,4,32,64,128]{4,3,2,1,0:T(8,128)(2,1)} %param.18) | copy-start | bytes 6291460
  0.6 1.7 copy-start.1
  2.4 1.2 copy-start.7
  6.5 39.6 %copy-start.10 = (bf16[128,512]{1,0:T(8,128)(2,1)S(1)}, bf16[128,512]{1,0:T(8,128)(2,1)}, u32[]{:S(2)}) copy-start(bf16[128,512]{1,0:T(8,128)(2,1)} %constant.78.clone.table_ref) | copy-start | bytes 393220
  6.6 52.4 %copy-start.16 = (bf16[256,1024]{1,0:T(8,128)(2,1)S(1)}, bf16[256,1024]{1,0:T(8,128)(2,1)}, u32[]{:S(2)}) copy-start(bf16[256,1024]{1,0:T(8,128)(2,1)} %constant.80.clone) | copy-start | bytes 1572868
  59.2 1.7 copy-start.14
  59.5 1.8 copy-start.18
  60.2 11.3 %copy-start.9 = (bf16[512,128]{1,0:T(8,128)(2,1)S(1)}, bf16[512,128]{1,0:T(8,128)(2,1)}, u32[]{:S(2)}) copy-start(bf16[512,128]{1,0:T(8,128)(2,1)} %constant.79.clone.table_ref) | copy-start | bytes 393220
  73.5 33.3 %all-to-all-start.3 = ((bf16[32,128,128]{2,1,0:T(8,128)(2,1)}), bf16[32,128,128]{2,1,0:T(8,128)(2,1)S(1)}, u32[]{:S(2)}, u32[]{:S(2)}) async-start(bf16[32,128,128]{2,1,0:T(8,128)(2,1)} %x_inverse.2), calls=%async_computation.3 | async-start | bytes 2097152 | tf_op jit(solution)/shard_map/all_to_all | solution.py:353
  79.1 1.6 copy-start.2
  80.7 3.3 %copy-start.23 = (f32[64]{0:T(128)S(1)}, f32[64]{0:T(128)}, u32[]{:S(2)}) copy-start(f32[64]{0:T(128)} %param.20) | copy-start | bytes 772
  80.7 3.4 %copy-start.22 = (bf16[64,64]{1,0:T(8,128)(2,1)S(1)}, bf16[64,64]{1,0:T(8,128)(2,1)}, u32[]{:S(2)}) copy-start(bf16[64,64]{1,0:T(8,128)(2,1)} %param.19) | copy-start | bytes 24580
  82.7 1.3 copy-start.5
  84.3 1.6 copy-start.3
  87.8 1.3 copy-start.6
  106.8 1.2 copy-start.11
  108.0 1.2 copy-start.12
  122.6 43.2 %copy-start.17 = (bf16[256,1024]{1,0:T(8,128)(2,1)S(1)}, bf16[256,1024]{1,0:T(8,128)(2,1)}, u32[]{:S(2)}) copy-start(bf16[256,1024]{1,0:T(8,128)(2,1)} %constant.80.clone) | copy-start | bytes 1572868
  165.8 3.3 %copy-start.15 = (bf16[1024,256]{1,0:T(8,128)(2,1)S(1)}, bf16[1024,256]{1,0:T(8,128)(2,1)}, u32[]{:S(2)}) copy-start(bf16[1024,256]{1,0:T(8,128)(2,1)} %constant.81.clone) | copy-start | bytes 1572868
  167.0 0.6 copy-start.20
  181.6 33.3 %all-to-all-start.7 = ((bf16[32,128,128]{2,1,0:T(8,128)(2,1)}), bf16[32,128,128]{2,1,0:T(8,128)(2,1)S(1)}, u32[]{:S(2)}, u32[]{:S(2)}) async-start(bf16[32,128,128]{2,1,0:T(8,128)(2,1)} %x_inverse.3), calls=%async_computation.7 | async-start | bytes 2097152 | tf_op jit(solution)/shard_map/all_to_all | solution.py:353
  187.2 1.6 copy-start.4
  188.8 2.8 %copy-start.19 = (bf16[2,4,32,2,64]{4,3,2,1,0:T(2,128)(2,1)S(1)}, bf16[2,4,32,2,64]{4,3,2,1,0:T(2,128)(2,1)}, u32[]{:S(2)}) copy-start(bf16[2,4,32,2,64]{4,3,2,1,0:T(2,128)(2,1)} %copy-done.18) | copy-start | bytes 196612
  188.8 2.8 %copy-start.21 = (bf16[1,4,32,2,128]{4,3,0,2,1:T(2,128)(2,1)S(1)}, bf16[1,4,32,2,128]{4,3,0,2,1:T(2,128)(2,1)}, u32[]{:S(2)}) copy-start(bf16[1,4,32,2,128]{4,3,0,2,1:T(2,128)(2,1)} %copy-done.20) | copy-start | bytes 196612
  214.8 1.2 copy-start.8
  216.1 1.6 copy-start.13
where the time goes:
time: 223 us; the launch traced here: 222 us
  blocking collectives  114 us (51%)
  waiting for transfers between devices  38.5 us (17%)
  Pallas kernels  33.5 us (15%)
  local copies, waits for them, and re-layouts  19.4 us (9%)
  starting transfers between devices  11.1 us (5%)
  matrix products  3.98 us (2%)
    all_to_all x6, blocking collectives, exchange(): return lax.all_to_all(x, axis, split_axis=0, concat_axis=0, tiled=True)  114 us
    all_to_all x2, waiting for transfers between devices, exchange(): return lax.all_to_all(x, axis, split_axis=0, concat_axis=0, tiled=True)  38.5 us
    unnamed x48, local copies, waits for them, and re-layouts  16.3 us
    pallas_call x1, Pallas kernels, middle(): call(middle_kernel, [jax.ShapeDtypeStruct((MY, PAIRS * ROWS, BC), BF), fl...  13.4 us
    all_to_all x2, starting transfers between devices, exchange(): return lax.all_to_all(x, axis, split_axis=0, concat_axis=0, tiled=True)  11.1 us
    pallas_call x1, Pallas kernels, last(): call(last_kernel, jax.ShapeDtypeStruct((BC, ZL * XL, NY), BF), (STEPS,),...  4.46 us
  transfers between devices with their start and end apart: 2, of which 2 were waited for; matrix products, arithmetic and copies ran while one was open for 1% of the time, Pallas kernels for 3%

commit v1 on v0

v1 whole, which is shorter than its diff:
```python
import functools
import math

import jax
import jax.numpy as jnp
import ml_dtypes
import numpy as np
from jax import lax
from jax.experimental import pallas as pl
from jax.experimental.pallas import tpu as pltpu
from jax.sharding import PartitionSpec as P

C = 64
NX = 128
NY = 128
NZ = 128
MX = 32
MY = 32
MZ = 32
BATCH = 2
GZ = 8
XY = 32
BC = BATCH * C
ZL = NZ // GZ
XL = NX // XY
ZP = 2
PAIRS = ZL // ZP
SUB = 2 * XL
ROWS = ZP * SUB
BF = jnp.bfloat16
F32 = jnp.float32
FORWARD = (NX * NY * NZ) ** (-0.5)
INVERSE = 0.5 * (MX * MY * MZ) ** (-0.5)


def rounded(values):
    return values.astype(np.float32).astype(ml_dtypes.bfloat16).astype(np.float32)


def cos_sin(length, modes, folded):
    freq = np.arange(modes)
    if folded:
        freq = np.where(freq < modes // 2, freq, length - modes + freq)
    phase = (np.arange(length)[:, None] * freq[None, :]) % length
    angle = phase.astype(np.float32) * np.float32(2.0 * math.pi / length)
    return rounded(np.cos(angle)), rounded(np.sin(angle))


@functools.lru_cache(maxsize=None)
def tables():
    cy, sy = cos_sin(NY, MY, False)
    cx, sx = cos_sin(NX, MX, True)
    cz, sz = cos_sin(NZ, MZ, True)
    same = np.eye(XL, dtype=np.float32)
    part = np.stack([cy, -sy])
    unit = np.einsum("ryk,xv->krxvy", part, same).reshape(MY * SUB, XL * NY)
    scale = np.where(np.arange(MY) == 0, 1.0, 2.0).astype(np.float32)
    doubled = unit * np.repeat(scale, SUB)[:, None]
    z2 = np.eye(ZP, dtype=np.float32)
    fx = np.stack([np.stack([cx, sx]), np.stack([-sx, cx])])
    fx = fx.reshape(2, 2, XY, XL, MX)
    x_fwd = np.einsum("sopvk,zw->kszpwov", fx, z2).reshape(MX * 2 * ZP, XY * ROWS)
    gx = np.stack([np.stack([cx, -sx]), np.stack([sx, cx])])
    gx = gx.reshape(2, 2, XY, XL, MX)
    x_inv = np.einsum("sopvk,zw->pzsvkow", gx, z2).reshape(XY * ROWS, MX * 2 * ZP)
    kx = MX // GZ
    kxe = np.eye(kx, dtype=np.float32)
    fz = np.stack([np.stack([cz, sz]), np.stack([-sz, cz])])
    fz = fz.reshape(2, 2, GZ, PAIRS, ZP, MZ)
    z_fwd = np.einsum("sogjzm,kl->skmgjloz", fz, kxe).reshape(2 * kx * MZ, GZ * PAIRS * kx * 2 * ZP)
    gz = np.stack([np.stack([cz, -sz]), np.stack([sz, cz])])
    gz = gz.reshape(2, 2, GZ, PAIRS, ZP, MZ)
    z_inv = np.einsum("sogjzm,kl->gjkszolm", gz, kxe).reshape(GZ * PAIRS * kx * 2 * ZP, 2 * kx * MZ)
    made = dict(
        unit=unit,
        doubled=doubled,
        doubled_t=doubled.T,
        x_fwd=x_fwd,
        x_inv=x_inv,
        z_fwd=z_fwd,
        z_inv=z_inv,
    )
    return {k: np.ascontiguousarray(v).astype(ml_dtypes.bfloat16) for k, v in made.items()}


def dot(a, b, dims=((1,), (0,))):
    return lax.dot_general(a, b, (dims, ((), ())), preferred_element_type=F32)


VM = 24 * 1024 * 1024
STEPS = PAIRS // 2
CELLS = ZP * XL
STEP_CELLS = 2 * CELLS
PLANE = XL * NY
VMEM = pl.BlockSpec(memory_space=pltpu.VMEM)
REMOTE = pl.BlockSpec(memory_space=pltpu.HBM)


def far(x):
    return pltpu.with_memory_space_constraint(x, pltpu.HBM)


def call(kernel, outs, in_specs, out_specs, scratch, name, flops, nbytes):
    return pl.pallas_call(
        kernel,
        out_shape=outs,
        in_specs=in_specs,
        out_specs=out_specs,
        scratch_shapes=scratch,
        name=name,
        compiler_params=pltpu.CompilerParams(vmem_limit_bytes=VM),
        cost_estimate=pl.CostEstimate(flops=flops, bytes_accessed=nbytes, transcendentals=0),
    )


def split_pair(block):
    wide = block.astype(F32)
    n = wide.shape[0]
    halves = [wide[:, z * SUB : (z + 1) * SUB, :].reshape(n * SUB, BC) for z in range(ZP)]
    return jnp.concatenate(halves, axis=1).astype(BF)


def join_pair(wide):
    n = wide.shape[0] // SUB
    halves = [wide[:, z * BC : (z + 1) * BC].reshape(n, SUB, BC) for z in range(ZP)]
    return jnp.concatenate(halves, axis=1).astype(BF)


def chunk_of(ref, step):
    return ref.at[:, step * STEP_CELLS : (step + 1) * STEP_CELLS, :]


def aligned(index, size):
    if isinstance(index, int):
        return index * size
    return pl.multiple_of(index * size, size)


def rows_of(ref, step):
    return ref.at[step * STEP_CELLS * NY : (step + 1) * STEP_CELLS * NY, :]


def first_kernel(x_ref, far_ref, out_ref, in_ref, table_ref, wide_ref, sem):
    copies = [
        pltpu.make_async_copy(chunk_of(x_ref, i), in_ref.at[i], sem.at[i]) for i in range(STEPS)
    ]
    fetch = pltpu.make_async_copy(far_ref, table_ref, sem.at[STEPS])
    copies[0].start()
    fetch.start()
    copies[1].start()
    for i in range(STEPS):
        copies[i].wait()
        if i + 2 < STEPS:
            copies[i + 2].start()
        if i == 0:
            fetch.wait()
        wide_ref[i % 2] = in_ref[i].astype(F32).reshape(BC * STEP_CELLS, NY)
        for j in range(2):
            planes = []
            for z in range(ZP):
                cells = [
                    wide_ref[i % 2, pl.ds(j * CELLS + z * XL + t, BC, stride=STEP_CELLS), :].astype(BF)
                    for t in range(XL)
                ]
                planes.append(jnp.concatenate(cells, axis=1))
            both = jnp.concatenate(planes, axis=0)
            modes = dot(table_ref[...], both, ((1,), (1,)))
            at = (2 * i + j) * ROWS
            out_ref[:, at : at + ROWS, :] = join_pair(modes)


def y_first(x, table):
    return call(
        first_kernel,
        jax.ShapeDtypeStruct((MY, PAIRS * ROWS, BC), BF),
        [REMOTE, REMOTE],
        VMEM,
        [
            pltpu.VMEM((STEPS, BC, STEP_CELLS, NY), BF),
            pltpu.VMEM(table.shape, BF),
            pltpu.VMEM((2, BC * STEP_CELLS, NY), F32),
            pltpu.SemaphoreType.DMA((STEPS + 1,)),
        ],
        "y_first",
        1 << 29,
        4 << 20,
    )(far(x), far(table))


def to_lanes_kernel(x_ref, out_ref, in_ref, made_ref, wide_ref, sem, out_sem):
    copies = [
        pltpu.make_async_copy(chunk_of(x_ref, i), in_ref.at[i], sem.at[i]) for i in range(STEPS)
    ]
    for copy in copies:
        copy.start()
    outs = []
    for i in range(STEPS):
        copies[i].wait()
        wide_ref[i % 2] = in_ref[i].astype(F32).reshape(BC * STEP_CELLS, NY)
        for t in range(STEP_CELLS):
            cell = wide_ref[i % 2, pl.ds(t, BC, stride=STEP_CELLS), :]
            made_ref[i, t * NY : (t + 1) * NY, :] = cell.T.astype(BF)
        outs.append(pltpu.make_async_copy(made_ref.at[i], rows_of(out_ref, i), out_sem.at[i]))
        outs[i].start()
    for copy in outs:
        copy.wait()


def to_lanes(x):
    return call(
        to_lanes_kernel,
        jax.ShapeDtypeStruct((ZL * XL * NY, BC), BF),
        [REMOTE],
        REMOTE,
        [
            pltpu.VMEM((STEPS, BC, STEP_CELLS, NY), BF),
            pltpu.VMEM((STEPS, STEP_CELLS * NY, BC), BF),
            pltpu.VMEM((2, BC * STEP_CELLS, NY), F32),
            pltpu.SemaphoreType.DMA((STEPS,)),
            pltpu.SemaphoreType.DMA((STEPS,)),
        ],
        "to_lanes",
        0,
        12 << 20,
    )(far(x))


def from_lanes_kernel(x_ref, out_ref, in_ref, made_ref, wide_ref, in_sem, sem):
    fetches = [
        pltpu.make_async_copy(rows_of(x_ref, i), in_ref.at[i], in_sem.at[i]) for i in range(STEPS)
    ]
    for copy in fetches:
        copy.start()
    copies = []
    for i in range(STEPS):
        fetches[i].wait()
        for t in range(STEP_CELLS):
            cell = in_ref[i, t * NY : (t + 1) * NY, :].astype(F32)
            wide_ref[i % 2, pl.ds(t, BC, stride=STEP_CELLS), :] = cell.T
        made_ref[i] = wide_ref[i % 2].reshape(BC, STEP_CELLS, NY).astype(BF)
        copies.append(pltpu.make_async_copy(made_ref.at[i], chunk_of(out_ref, i), sem.at[i]))
        copies[i].start()
    for copy in copies:
        copy.wait()


def from_lanes(x):
    return call(
        from_lanes_kernel,
        jax.ShapeDtypeStruct((BC, ZL * XL, NY), BF),
        [REMOTE],
        REMOTE,
        [
            pltpu.VMEM((STEPS, STEP_CELLS * NY, BC), BF),
            pltpu.VMEM((STEPS, BC, STEP_CELLS, NY), BF),
            pltpu.VMEM((2, BC * STEP_CELLS, NY), F32),
            pltpu.SemaphoreType.DMA((STEPS,)),
            pltpu.SemaphoreType.DMA((STEPS,)),
        ],
        "from_lanes",
        0,
        12 << 20,
    )(far(x))


def x_kernel(groups_in, groups_out, scale, recv_ref, table_ref, out_ref):
    for i in range(STEPS):
        wide = jnp.concatenate(
            [
                recv_ref[:, (2 * i + j) * ROWS : (2 * i + j + 1) * ROWS, :].reshape(
                    groups_in * ROWS, BC
                )
                for j in range(2)
            ],
            axis=1,
        )
        done = (dot(table_ref[...], wide) * scale).astype(BF)
        for j in range(2):
            at = (2 * i + j) * ROWS
            out_ref[:, at : at + ROWS, :] = done[:, j * BC : (j + 1) * BC].reshape(
                groups_out, ROWS, BC
            )


def x_transform(recv, table, groups_out, scale, name):
    return call(
        functools.partial(x_kernel, recv.shape[0], groups_out, scale),
        jax.ShapeDtypeStruct((groups_out, PAIRS * ROWS, BC), BF),
        [VMEM, VMEM],
        VMEM,
        [],
        name,
        1 << 27,
        2 << 20,
    )(recv, table)


def middle_kernel(
    recv_ref,
    x_far,
    cot_far,
    inv_far,
    fwd_far,
    mix_ref,
    bias_ref,
    send_ref,
    layer_ref,
    pre_ref,
    x_ref,
    cot_ref,
    inv_ref,
    fwd_ref,
    cat_ref,
    x_sem,
    cot_sem,
    table_sem,
):
    depth = ZP * PLANE

    def part(ref, pair):
        return ref.at[pl.ds(aligned(pair, depth), depth), :]

    def move(source, target, sem, pair):
        return pltpu.make_async_copy(part(source, pair), part(target, pair), sem.at[pair])

    tables = [
        pltpu.make_async_copy(inv_far, inv_ref, table_sem.at[0]),
        pltpu.make_async_copy(fwd_far, fwd_ref, table_sem.at[1]),
    ]

    def fetch(pair):
        move(x_far, x_ref, x_sem, pair).start()
        move(cot_far, cot_ref, cot_sem, pair).start()

    tables[0].start()
    fetch(0)
    tables[1].start()
    fetch(1)

    def forward(pair):
        modes = dot(fwd_ref[...], cat_ref[pair & 1])
        send_ref[:, pl.ds(aligned(pair, ROWS), ROWS), :] = join_pair(modes)

    mix = mix_ref[...]
    none = jnp.zeros_like(mix)
    lower = jnp.concatenate(
        [jnp.concatenate([mix, none], axis=1), jnp.concatenate([none, mix], axis=1)], axis=0
    )
    bias = bias_ref[...]

    tables[0].wait()

    def step(pair, first=False, final=False):
        if not final:
            fetch(pair + 2)
        if not first:
            forward(pair - 1)
        block = recv_ref[:, pl.ds(aligned(pair, ROWS), ROWS), :]
        right = jnp.concatenate([split_pair(block), lower], axis=0)
        base = aligned(pair, depth)
        move(x_far, x_ref, x_sem, pair).wait()
        move(cot_far, cot_ref, cot_sem, pair).wait()
        for t in range(XL):
            cells = [pl.ds(base + z * PLANE + t * NY, NY) for z in range(ZP)]
            left = jnp.concatenate(
                [inv_ref[t * NY : (t + 1) * NY, :]] + [x_ref[rows, :] for rows in cells], axis=1
            )
            total = dot(left, right)
            for z, rows in enumerate(cells):
                p = total[:, z * BC : (z + 1) * BC] + bias
                square = p * p
                inner = 0.7978845608 + (0.7978845608 * 0.044715) * square
                half = 0.5 + 0.5 * jnp.tanh(p * inner)
                layer_ref[rows, :] = (p * half).astype(BF)
                tail = (2.0 * 0.7978845608) + (6.0 * 0.7978845608 * 0.044715) * square
                slope = half + half * (1.0 - half) * (p * tail)
                grad = (cot_ref[rows, :].astype(F32) * slope).astype(BF)
                pre_ref[rows, :] = grad
                cat_ref[pair & 1, t * NY : (t + 1) * NY, z * BC : (z + 1) * BC] = grad

    def steps(pair, carry):
        step(pair)
        return carry

    step(0, first=True)
    tables[1].wait()
    lax.fori_loop(1, PAIRS - 3, steps, 0, unroll=2)
    step(PAIRS - 3)
    step(PAIRS - 2, final=True)
    step(PAIRS - 1, final=True)
    forward(PAIRS - 1)


def middle(recv, x, cot, inv, fwd, mix, bias):
    cells = (ZL * XL * NY, BC)
    flat = jax.ShapeDtypeStruct(cells, BF)
    return call(
        middle_kernel,
        [jax.ShapeDtypeStruct((MY, PAIRS * ROWS, BC), BF), flat, flat],
        [VMEM] + [REMOTE] * 4 + [VMEM] * 2,
        [VMEM] * 3,
        [
            pltpu.VMEM(cells, BF),
            pltpu.VMEM(cells, BF),
            pltpu.VMEM(inv.shape, BF),
            pltpu.VMEM(fwd.shape, BF),
            pltpu.VMEM((2, PLANE, ZP * BC), BF),
            pltpu.SemaphoreType.DMA((PAIRS,)),
            pltpu.SemaphoreType.DMA((PAIRS,)),
            pltpu.SemaphoreType.DMA((2,)),
        ],
        "middle",
        2 << 29,
        12 << 20,
    )(recv, far(x), far(cot), far(inv), far(fwd), mix, bias)


def last_kernel(recv_ref, pre_ref, inv_ref, mix_ref, out_ref, in_ref, made_ref, wide_ref, in_sem, sem):
    fetches = [
        pltpu.make_async_copy(rows_of(pre_ref, i), in_ref.at[i], in_sem.at[i]) for i in range(STEPS)
    ]
    for copy in fetches[:2]:
        copy.start()
    copies = []
    for i in range(STEPS):
        for j in range(2):
            pair = 2 * i + j
            modes = split_pair(recv_ref[:, pair * ROWS : (pair + 1) * ROWS, :])
            cells = dot(modes, inv_ref[...], ((0,), (0,)))
            if j == 0:
                fetches[i].wait()
                if i + 2 < STEPS:
                    fetches[i + 2].start()
            rows = in_ref[i, j * ZP * PLANE : (j + 1) * ZP * PLANE, :]
            local = dot(mix_ref[...], rows, ((1,), (1,)))
            for z in range(ZP):
                for t in range(XL):
                    at = z * XL + t
                    wide_ref[i % 2, pl.ds(j * CELLS + at, BC, stride=STEP_CELLS), :] = (
                        cells[z * BC : (z + 1) * BC, t * NY : (t + 1) * NY]
                        + local[:, at * NY : (at + 1) * NY]
                    )
        made_ref[i] = wide_ref[i % 2].reshape(BC, STEP_CELLS, NY).astype(BF)
        copies.append(pltpu.make_async_copy(made_ref.at[i], chunk_of(out_ref, i), sem.at[i]))
        copies[i].start()
    for copy in copies:
        copy.wait()


def last(recv, pre, inv, mix):
    return call(
        last_kernel,
        jax.ShapeDtypeStruct((BC, ZL * XL, NY), BF),
        [VMEM, REMOTE, VMEM, VMEM],
        REMOTE,
        [
            pltpu.VMEM((STEPS, STEP_CELLS * NY, BC), BF),
            pltpu.VMEM((STEPS, BC, STEP_CELLS, NY), BF),
            pltpu.VMEM((2, BC * STEP_CELLS, NY), F32),
            pltpu.SemaphoreType.DMA((STEPS,)),
            pltpu.SemaphoreType.DMA((STEPS,)),
        ],
        "last",
        2 << 29,
        8 << 20,
    )(recv, far(pre), inv, mix)


def exchange(x, axis):
    return lax.all_to_all(x, axis, split_axis=0, concat_axis=0, tiled=True)


KX = MX // GZ


def z_forward(recv, table):
    modes = dot(table, recv.reshape(GZ * PAIRS * ROWS, BC))
    return modes.astype(BF).reshape(2, KX, MZ, BATCH, C)


def z_inverse(modes, table):
    return dot(table, modes.reshape(2 * KX * MZ, BC)).astype(BF).reshape(GZ, PAIRS * ROWS, BC)


def body(features, cotangent, spectral, pointwise, channel_bias):
    t = {k: jnp.asarray(v) for k, v in tables().items()}
    x = features.reshape(BC, ZL * XL, NY)
    cot = cotangent.reshape(BC, ZL * XL, NY)
    weights = spectral[0]
    mix = jnp.zeros((BATCH, C, BATCH, C), BF)
    mix = mix.at[0, :, 0, :].set(pointwise).at[1, :, 1, :].set(pointwise).reshape(BC, BC)
    bias = jnp.tile(channel_bias, BATCH)[None, :]

    recv = exchange(y_first(x, t["unit"]), "xy")
    x_lanes = to_lanes(x)
    recv = exchange(x_transform(recv, t["x_fwd"], GZ, FORWARD, "x_forward"), "gz")
    spectra = z_forward(recv, t["z_fwd"])
    products = jnp.einsum("rkmbi,kmio->rkmbo", spectra, weights, preferred_element_type=F32)
    mixed = jnp.stack(
        [
            products[0, ..., :C] - products[1, ..., C:],
            products[0, ..., C:] + products[1, ..., :C],
        ]
    ).astype(BF)
    recv = exchange(z_inverse(mixed, t["z_inv"]), "gz")
    recv = exchange(x_transform(recv, t["x_inv"], XY, INVERSE, "x_inverse"), "xy")
    cot_lanes = to_lanes(cot)
    send, layer, pre = middle(
        recv, x_lanes, cot_lanes, t["doubled_t"], t["doubled"], mix, bias
    )
    recv = exchange(send, "xy")
    layer_out = from_lanes(layer)
    recv = exchange(x_transform(recv, t["x_fwd"], GZ, INVERSE, "x_forward"), "gz")
    mode_grad = z_forward(recv, t["z_fwd"])
    real, imag = mode_grad[0], mode_grad[1]
    paired = jnp.stack(
        [
            jnp.concatenate([real, imag], axis=-1),
            jnp.concatenate([imag, -real], axis=-1),
        ]
    )
    spectra_grad = jnp.einsum(
        "rkmbo,kmio->rkmbi", paired, weights, preferred_element_type=F32
    ).astype(BF)
    recv = exchange(z_inverse(spectra_grad, t["z_inv"]), "gz")
    recv = exchange(x_transform(recv, t["x_inv"], XY, FORWARD, "x_inverse"), "xy")
    spectral_grad = jnp.einsum(
        "rkmbi,rkmbo->kmio", spectra, paired, preferred_element_type=F32
    ).astype(BF)
    input_grad = last(recv, pre, t["unit"], mix)
    return (
        layer_out.reshape(features.shape),
        input_grad.reshape(features.shape),
        spectral_grad[None],
    )


def solution(mesh):
    field = P(None, None, "gz", "xy", None)
    modes = P("xy", "gz", None, None, None)
    return jax.shard_map(
        body,
        mesh=mesh,
        in_specs=(field, field, modes, P(), P()),
        out_specs=(field, field, modes),
        check_vma=False,
    )
```

time: 223 us -> 207 us (0.928)
  local copies, waits for them, and re-layouts: 19.4 us -> 6.47 us
  Pallas kernels: 33.5 us -> 28.2 us
    unnamed x48 -> x36, local copies, waits for them, and re-layouts: 16.3 us -> 3.32 us
    pallas_call x1, Pallas kernels: 13.4 us -> 7.67 us  [middle(): call(middle_kernel, [jax.ShapeDtypeStruct((MY, PAIRS * ROWS, BC), BF), fl...]
  transfers between devices with their start and end apart: 2 -> 2, of which waited for: 2 -> 2; matrix products, arithmetic and copies ran while one was open for 1% -> 1% of each run, Pallas kernels for 3% -> 5%
where the time goes in v1:
time: 207 us; the launch traced here: 206 us
  blocking collectives  114 us (55%)
  waiting for transfers between devices  40.6 us (20%)
  Pallas kernels  28.2 us (14%)
  starting transfers between devices  11.1 us (5%)
  local copies, waits for them, and re-layouts  6.47 us (3%)
  matrix products  3.98 us (2%)
    all_to_all x6, blocking collectives, exchange(): return lax.all_to_all(x, axis, split_axis=0, concat_axis=0, tiled=True)  114 us
    all_to_all x2, waiting for transfers between devices, exchange(): return lax.all_to_all(x, axis, split_axis=0, concat_axis=0, tiled=True)  40.6 us
    all_to_all x2, starting transfers between devices, exchange(): return lax.all_to_all(x, axis, split_axis=0, concat_axis=0, tiled=True)  11.1 us
    pallas_call x1, Pallas kernels, middle(): call(middle_kernel, [jax.ShapeDtypeStruct((MY, PAIRS * ROWS, BC), BF), fl...  7.67 us
    pallas_call x2, Pallas kernels, to_lanes(): call(to_lanes_kernel, jax.ShapeDtypeStruct((ZL * XL * NY, BC), BF), [REMO...  5.81 us
    pallas_call x1, Pallas kernels, last(): call(last_kernel, jax.ShapeDtypeStruct((BC, ZL * XL, NY), BF), [VMEM, REM...  4.31 us
  transfers between devices with their start and end apart: 2, of which 2 were waited for; matrix products, arithmetic and copies ran while one was open for 1% of the time, Pallas kernels for 5%

profile of v1, /device:TPU:2, one launch (start us, length us, event | category | flops | bytes accessed | tf_op | source)
XLA Modules:
  0.0 206.2 jit_solution(1692922641874436447)
XLA Ops:
  0.7 3.5 %y_first.1 = bf16[32,128,128]{2,1,0:T(8,128)(2,1)S(1)} custom-call(bf16[128,64,128]{2,1,0:T(8,128)(2,1)} %bitcast.56, bf16[256,512]{1,0:T(8,128)(2,1)} %constant.75.clone.far_ref.inv_ref), custom_call_target="tpu_custom_call" | custom-call | flops 536870912 | bytes 4194304 | tf_op jit(solution)/shard_map/y_first/pallas_call | solution.py:173
  4.2 39.6 %all_to_all.40.recv_ref = bf16[32,128,128]{2,1,0:T(8,128)(2,1)S(1)} all-to-all(bf16[32,128,128]{2,1,0:T(8,128)(2,1)S(1)} %y_first.1), channel_id=1, replica_groups=mesh['gz'=8,'xy'=32] {'xy'}, dimensions={0} | all-to-all | bytes 2097152 | tf_op jit(solution)/shard_map/all_to_all | solution.py:470
  43.8 0.3 x_forward.2
  44.1 11.8 %all_to_all.41 = bf16[8,128,128]{2,1,0:T(8,128)(2,1)S(1)} all-to-all(bf16[8,128,128]{2,1,0:T(8,128)(2,1)S(1)} %x_forward.2), channel_id=1, replica_groups=mesh['gz'=8,'xy'=32] {'gz'}, dimensions={0} | all-to-all | bytes 524288 | tf_op jit(solution)/shard_map/all_to_all | solution.py:470
  55.9 0.3 fusion.16
  56.3 0.1 copy.25
  56.4 0.1 reshape.123
  56.5 0.7 fusion.7
  57.2 0.3 fusion.19
  57.5 0.2 pad_maximum_fusion
  57.8 0.1 copy.27
  57.9 0.1 convert_element_type.40
  58.0 0.3 fusion.5
  58.3 0.2 copy.28
  58.5 9.9 %all_to_all.42.recv_ref = bf16[8,128,128]{2,1,0:T(8,128)(2,1)S(1)} all-to-all(bf16[8,128,128]{2,1,0:T(8,128)(2,1)S(1)} %bitcast.64), channel_id=1, replica_groups=mesh['gz'=8,'xy'=32] {'gz'}, dimensions={0} | all-to-all | bytes 524288 | tf_op jit(solution)/shard_map/all_to_all | solution.py:470
  68.4 1.4 x_inverse.2
  69.8 5.6 %all-to-all-start.3 = ((bf16[32,128,128]{2,1,0:T(8,128)(2,1)}), bf16[32,128,128]{2,1,0:T(8,128)(2,1)S(1)}, u32[]{:S(2)}, u32[]{:S(2)}) async-start(bf16[32,128,128]{2,1,0:T(8,128)(2,1)} %x_inverse.2), calls=%async_computation.3 | async-start | bytes 2097152 | tf_op jit(solution)/shard_map/all_to_all | solution.py:470
  75.4 2.9 %to_lanes.2.x_far = bf16[8192,128]{1,0:T(8,128)(2,1)S(1)} custom-call(bf16[128,64,128]{2,1,0:T(8,128)(2,1)} %bitcast.57), custom_call_target="tpu_custom_call" | custom-call | bytes 12582912 | tf_op jit(solution)/shard_map/to_lanes/pallas_call | solution.py:210
  78.4 1.3 copy-done.1
  79.7 0.1 broadcast_in_dim_tile.3.bias_ref
  79.9 0.1 reshape.127.mix_ref
  80.0 2.9 %to_lanes.3.cot_far = bf16[8192,128]{1,0:T(8,128)(2,1)S(1)} custom-call(bf16[128,64,128]{2,1,0:T(8,128)(2,1)} %bitcast.58), custom_call_target="tpu_custom_call" | custom-call | bytes 12582912 | tf_op jit(solution)/shard_map/to_lanes/pallas_call | solution.py:210
  82.9 1.3 copy-done.2
  84.2 18.9 %all-to-all-done.3.recv_ref = bf16[32,128,128]{2,1,0:T(8,128)(2,1)S(1)} async-done(((bf16[32,128,128]{2,1,0:T(8,128)(2,1)}), bf16[32,128,128]{2,1,0:T(8,128)(2,1)S(1)}, u32[]{:S(2)}, u32[]{:S(2)}) %all-to-all-start.3) | async-done | bytes 1048608 | tf_op jit(solution)/shard_map/all_to_all | solution.py:470
  103.1 7.7 %middle.1 = (bf16[32,128,128]{2,1,0:T(8,128)(2,1)S(1)}, bf16[8192,128]{1,0:T(8,128)(2,1)S(1)}, bf16[8192,128]{1,0:T(8,128)(2,1)S(1)}) custom-call(bf16[32,128,128]{2,1,0:T(8,128)(2,1)S(1)} %all-to-all-done.3.recv_ref, bf16[8192,128]{1,0:T(8,128)(2,1)} %copy-done.1, bf16[8192,128]{1,0:T(8,128)(2,1)} %copy-done.2, bf16[512,256]{1,0:T(8,128)(2,1)} %constant.77.clone.inv_far, ...), custom_call_target="tpu_custom_call" | custom-call | flops 1073741824 | bytes 12582912 | tf_op jit(solution)/shard_map/middle/pallas_call | solution.py:397
  110.8 32.2 %all_to_all.43.recv_ref = bf16[32,128,128]{2,1,0:T(8,128)(2,1)S(1)} all-to-all(bf16[32,128,128]{2,1,0:T(8,128)(2,1)S(1)} %get-tuple-element.31), channel_id=1, replica_groups=mesh['gz'=8,'xy'=32] {'xy'}, dimensions={0} | all-to-all | bytes 2097152 | tf_op jit(solution)/shard_map/all_to_all | solution.py:470
  143.1 0.3 x_forward.3
  143.4 10.0 %all_to_all.44 = bf16[8,128,128]{2,1,0:T(8,128)(2,1)S(1)} all-to-all(bf16[8,128,128]{2,1,0:T(8,128)(2,1)S(1)} %x_forward.3), channel_id=1, replica_groups=mesh['gz'=8,'xy'=32] {'gz'}, dimensions={0} | all-to-all | bytes 524288 | tf_op jit(solution)/shard_map/all_to_all | solution.py:470
  153.4 0.3 fusion.17
  153.7 0.1 copy.31
  153.9 0.1 squeeze.15
  154.0 0.1 copy.30
  154.1 0.1 squeeze.14
  154.2 0.4 maximum_bitcast_fusion
  154.6 0.6 copy-done.14
  155.2 1.2 fusion.13
  156.4 0.1 copy.32
  156.5 0.1 reshape.130
  156.7 0.3 fusion.6
  157.0 0.2 copy.33
  157.1 9.9 %all_to_all.45.recv_ref = bf16[8,128,128]{2,1,0:T(8,128)(2,1)S(1)} all-to-all(bf16[8,128,128]{2,1,0:T(8,128)(2,1)S(1)} %bitcast.65), channel_id=1, replica_groups=mesh['gz'=8,'xy'=32] {'gz'}, dimensions={0} | all-to-all | bytes 524288 | tf_op jit(solution)/shard_map/all_to_all | solution.py:470
  167.1 1.4 x_inverse.3
  168.5 5.6 %all-to-all-start.7 = ((bf16[32,128,128]{2,1,0:T(8,128)(2,1)}), bf16[32,128,128]{2,1,0:T(8,128)(2,1)S(1)}, u32[]{:S(2)}, u32[]{:S(2)}) async-start(bf16[32,128,128]{2,1,0:T(8,128)(2,1)} %x_inverse.3), calls=%async_computation.7 | async-start | bytes 2097152 | tf_op jit(solution)/shard_map/all_to_all | solution.py:470
  174.1 3.5 %from_lanes.1 = bf16[128,64,128]{2,1,0:T(8,128)(2,1)} custom-call(bf16[8192,128]{1,0:T(8,128)(2,1)} %copy-done.4), custom_call_target="tpu_custom_call" | custom-call | bytes 12582912 | tf_op jit(solution)/shard_map/from_lanes/pallas_call | solution.py:248
  177.6 0.9 fusion.20
  178.5 1.5 copy.51
  180.0 21.7 %all-to-all-done.7.recv_ref = bf16[32,128,128]{2,1,0:T(8,128)(2,1)S(1)} async-done(((bf16[32,128,128]{2,1,0:T(8,128)(2,1)}), bf16[32,128,128]{2,1,0:T(8,128)(2,1)S(1)}, u32[]{:S(2)}, u32[]{:S(2)}) %all-to-all-start.7) | async-done | bytes 1048608 | tf_op jit(solution)/shard_map/all_to_all | solution.py:470
  201.7 4.3 %last.1 = bf16[128,64,128]{2,1,0:T(8,128)(2,1)} custom-call(bf16[32,128,128]{2,1,0:T(8,128)(2,1)S(1)} %all-to-all-done.7.recv_ref, bf16[8192,128]{1,0:T(8,128)(2,1)} %copy-done.3, bf16[256,512]{1,0:T(8,128)(2,1)S(1)} %copy-done.5, bf16[128,128]{1,0:T(8,128)(2,1)S(1)} %reshape.127.mix_ref), custom_call_target="tpu_custom_call" | custom-call | flops 1073741824 | bytes 8388608 | tf_op jit(solution)/shard_map/last/pallas_call | solution.py:451
  (39 shorter events, 0.3 us)
Async XLA Ops:
  0.6 55.9 %copy-start = (bf16[1,4,32,64,128]{4,3,2,1,0:T(8,128)(2,1)S(1)}, bf16[1,4,32,64,128]{4,3,2,1,0:T(8,128)(2,1)}, u32[]{:S(2)}) copy-start(bf16[1,4,32,64,128]{4,3,2,1,0:T(8,128)(2,1)} %param.18) | copy-start | bytes 6291460
  0.6 43.2 %copy-start.7 = (bf16[128,512]{1,0:T(8,128)(2,1)S(1)}, bf16[128,512]{1,0:T(8,128)(2,1)}, u32[]{:S(2)}) copy-start(bf16[128,512]{1,0:T(8,128)(2,1)} %constant.78.clone.table_ref) | copy-start | bytes 393220
  4.2 51.8 %copy-start.10 = (bf16[256,1024]{1,0:T(8,128)(2,1)S(1)}, bf16[256,1024]{1,0:T(8,128)(2,1)}, u32[]{:S(2)}) copy-start(bf16[256,1024]{1,0:T(8,128)(2,1)} %constant.80.clone) | copy-start | bytes 1572868
  56.3 1.7 copy-start.8
  56.5 1.8 copy-start.12
  57.2 11.3 %copy-start.6 = (bf16[512,128]{1,0:T(8,128)(2,1)S(1)}, bf16[512,128]{1,0:T(8,128)(2,1)}, u32[]{:S(2)}) copy-start(bf16[512,128]{1,0:T(8,128)(2,1)} %constant.79.clone.table_ref) | copy-start | bytes 393220
  69.8 33.3 %all-to-all-start.3 = ((bf16[32,128,128]{2,1,0:T(8,128)(2,1)}), bf16[32,128,128]{2,1,0:T(8,128)(2,1)S(1)}, u32[]{:S(2)}, u32[]{:S(2)}) async-start(bf16[32,128,128]{2,1,0:T(8,128)(2,1)} %x_inverse.2), calls=%async_computation.3 | async-start | bytes 2097152 | tf_op jit(solution)/shard_map/all_to_all | solution.py:470
  75.4 4.3 %copy-start.17 = (f32[64]{0:T(128)S(1)}, f32[64]{0:T(128)}, u32[]{:S(2)}) copy-start(f32[64]{0:T(128)} %param.20) | copy-start | bytes 772
  75.4 4.3 %copy-start.16 = (bf16[64,64]{1,0:T(8,128)(2,1)S(1)}, bf16[64,64]{1,0:T(8,128)(2,1)}, u32[]{:S(2)}) copy-start(bf16[64,64]{1,0:T(8,128)(2,1)} %param.19) | copy-start | bytes 24580
  78.4 1.3 copy-start.1
  82.9 1.3 copy-start.2
  110.8 42.9 %copy-start.3 = (bf16[8192,128]{1,0:T(8,128)(2,1)}, bf16[8192,128]{1,0:T(8,128)(2,1)S(1)}, u32[]{:S(2)}) copy-start(bf16[8192,128]{1,0:T(8,128)(2,1)S(1)} %get-tuple-element.32.pre_ref) | copy-start | bytes 6291460
  110.8 42.9 %copy-start.4 = (bf16[8192,128]{1,0:T(8,128)(2,1)}, bf16[8192,128]{1,0:T(8,128)(2,1)S(1)}, u32[]{:S(2)}) copy-start(bf16[8192,128]{1,0:T(8,128)(2,1)S(1)} %get-tuple-element.30.x_ref) | copy-start | bytes 6291460
  110.8 42.6 %copy-start.11 = (bf16[256,1024]{1,0:T(8,128)(2,1)S(1)}, bf16[256,1024]{1,0:T(8,128)(2,1)}, u32[]{:S(2)}) copy-start(bf16[256,1024]{1,0:T(8,128)(2,1)} %constant.80.clone) | copy-start | bytes 1572868
  153.4 3.3 %copy-start.9 = (bf16[1024,256]{1,0:T(8,128)(2,1)S(1)}, bf16[1024,256]{1,0:T(8,128)(2,1)}, u32[]{:S(2)}) copy-start(bf16[1024,256]{1,0:T(8,128)(2,1)} %constant.81.clone) | copy-start | bytes 1572868
  154.6 0.6 copy-start.14
  168.5 33.3 %all-to-all-start.7 = ((bf16[32,128,128]{2,1,0:T(8,128)(2,1)}), bf16[32,128,128]{2,1,0:T(8,128)(2,1)S(1)}, u32[]{:S(2)}, u32[]{:S(2)}) async-start(bf16[32,128,128]{2,1,0:T(8,128)(2,1)} %x_inverse.3), calls=%async_computation.7 | async-start | bytes 2097152 | tf_op jit(solution)/shard_map/all_to_all | solution.py:470
  174.1 3.5 %copy-start.13 = (bf16[2,4,32,2,64]{4,3,2,1,0:T(2,128)(2,1)S(1)}, bf16[2,4,32,2,64]{4,3,2,1,0:T(2,128)(2,1)}, u32[]{:S(2)}) copy-start(bf16[2,4,32,2,64]{4,3,2,1,0:T(2,128)(2,1)} %copy-done.12) | copy-start | bytes 196612
  174.1 3.5 %copy-start.15 = (bf16[1,4,32,2,128]{4,3,0,2,1:T(2,128)(2,1)S(1)}, bf16[1,4,32,2,128]{4,3,0,2,1:T(2,128)(2,1)}, u32[]{:S(2)}) copy-start(bf16[1,4,32,2,128]{4,3,0,2,1:T(2,128)(2,1)} %copy-done.14) | copy-start | bytes 196612
  178.5 23.2 %copy-start.5 = (bf16[256,512]{1,0:T(8,128)(2,1)S(1)}, bf16[256,512]{1,0:T(8,128)(2,1)}, u32[]{:S(2)}) copy-start(bf16[256,512]{1,0:T(8,128)(2,1)} %constant.75.clone.far_ref.inv_ref) | copy-start | bytes 786436

commit v2 on v1

--- a/solution.py
+++ b/solution.py
@@ -141,20 +141,21 @@
 
 
 def first_kernel(x_ref, far_ref, out_ref, in_ref, table_ref, wide_ref, sem):
+    cells = [pl.ds(0, STEP_CELLS), pl.ds(STEP_CELLS, ZL * XL - STEP_CELLS)]
     copies = [
-        pltpu.make_async_copy(chunk_of(x_ref, i), in_ref.at[i], sem.at[i]) for i in range(STEPS)
+        pltpu.make_async_copy(x_ref.at[:, part, :], in_ref.at[:, part, :], sem.at[k])
+        for k, part in enumerate(cells)
     ]
-    fetch = pltpu.make_async_copy(far_ref, table_ref, sem.at[STEPS])
+    fetch = pltpu.make_async_copy(far_ref, table_ref, sem.at[2])
     copies[0].start()
     fetch.start()
     copies[1].start()
     for i in range(STEPS):
-        copies[i].wait()
-        if i + 2 < STEPS:
-            copies[i + 2].start()
+        if i < 2:
+            copies[i].wait()
         if i == 0:
             fetch.wait()
-        wide_ref[i % 2] = in_ref[i].astype(F32).reshape(BC * STEP_CELLS, NY)
+        wide_ref[i % 2] = in_ref[:, i * STEP_CELLS : (i + 1) * STEP_CELLS, :].astype(F32).reshape(BC * STEP_CELLS, NY)
         for j in range(2):
             planes = []
             for z in range(ZP):
@@ -176,10 +177,10 @@
         [REMOTE, REMOTE],
         VMEM,
         [
-            pltpu.VMEM((STEPS, BC, STEP_CELLS, NY), BF),
+            pltpu.VMEM((BC, ZL * XL, NY), BF),
             pltpu.VMEM(table.shape, BF),
             pltpu.VMEM((2, BC * STEP_CELLS, NY), F32),
-            pltpu.SemaphoreType.DMA((STEPS + 1,)),
+            pltpu.SemaphoreType.DMA((3,)),
         ],
         "y_first",
         1 << 29,
@@ -263,7 +264,9 @@
     )(far(x))
 
 
-def x_kernel(groups_in, groups_out, scale, recv_ref, table_ref, out_ref):
+def x_kernel(groups_in, groups_out, scale, recv_ref, table_ref, out_ref, made_ref=None, sem=None):
+    target = out_ref if made_ref is None else made_ref
+    copies = []
     for i in range(STEPS):
         wide = jnp.concatenate(
             [
@@ -277,22 +280,34 @@
         done = (dot(table_ref[...], wide) * scale).astype(BF)
         for j in range(2):
             at = (2 * i + j) * ROWS
-            out_ref[:, at : at + ROWS, :] = done[:, j * BC : (j + 1) * BC].reshape(
+            target[:, at : at + ROWS, :] = done[:, j * BC : (j + 1) * BC].reshape(
                 groups_out, ROWS, BC
             )
-
-
-def x_transform(recv, table, groups_out, scale, name):
+        if made_ref is not None and i % 2 == 1:
+            rows = pl.ds((i - 1) * 2 * ROWS, 4 * ROWS)
+            copies.append(
+                pltpu.make_async_copy(made_ref.at[:, rows, :], out_ref.at[:, rows, :], sem.at[i // 2])
+            )
+            copies[-1].start()
+    for copy in copies:
+        copy.wait()
+
+
+def x_transform(recv, table, groups_out, scale, name, away=False):
+    shape = (groups_out, PAIRS * ROWS, BC)
     return call(
         functools.partial(x_kernel, recv.shape[0], groups_out, scale),
-        jax.ShapeDtypeStruct((groups_out, PAIRS * ROWS, BC), BF),
+        jax.ShapeDtypeStruct(shape, BF),
         [VMEM, VMEM],
-        VMEM,
-        [],
+        REMOTE if away else VMEM,
+        [pltpu.VMEM(shape, BF), pltpu.SemaphoreType.DMA((STEPS // 2,))] if away else [],
         name,
         1 << 27,
         2 << 20,
     )(recv, table)
+
+
+GROUPS = ((0, 1), (1, 3), (3, PAIRS))
 
 
 def middle_kernel(
@@ -317,25 +332,25 @@
 ):
     depth = ZP * PLANE
 
-    def part(ref, pair):
-        return ref.at[pl.ds(aligned(pair, depth), depth), :]
-
-    def move(source, target, sem, pair):
-        return pltpu.make_async_copy(part(source, pair), part(target, pair), sem.at[pair])
+    def moves(group):
+        low, high = GROUPS[group]
+        rows = pl.ds(low * depth, (high - low) * depth)
+        return [
+            pltpu.make_async_copy(source.at[rows, :], target.at[rows, :], sem.at[group])
+            for source, target, sem in ((x_far, x_ref, x_sem), (cot_far, cot_ref, cot_sem))
+        ]
 
     tables = [
         pltpu.make_async_copy(inv_far, inv_ref, table_sem.at[0]),
         pltpu.make_async_copy(fwd_far, fwd_ref, table_sem.at[1]),
     ]
 
-    def fetch(pair):
-        move(x_far, x_ref, x_sem, pair).start()
-        move(cot_far, cot_ref, cot_sem, pair).start()
-
     tables[0].start()
-    fetch(0)
-    tables[1].start()
-    fetch(1)
+    for group in range(len(GROUPS)):
+        for move in moves(group):
+            move.start()
+        if group == 0:
+            tables[1].start()
 
     def forward(pair):
         modes = dot(fwd_ref[...], cat_ref[pair & 1])
@@ -350,16 +365,12 @@
 
     tables[0].wait()
 
-    def step(pair, first=False, final=False):
-        if not final:
-            fetch(pair + 2)
+    def step(pair, first=False):
         if not first:
             forward(pair - 1)
         block = recv_ref[:, pl.ds(aligned(pair, ROWS), ROWS), :]
         right = jnp.concatenate([split_pair(block), lower], axis=0)
         base = aligned(pair, depth)
-        move(x_far, x_ref, x_sem, pair).wait()
-        move(cot_far, cot_ref, cot_sem, pair).wait()
         for t in range(XL):
             cells = [pl.ds(base + z * PLANE + t * NY, NY) for z in range(ZP)]
             left = jnp.concatenate(
@@ -382,12 +393,17 @@
         step(pair)
         return carry
 
-    step(0, first=True)
-    tables[1].wait()
-    lax.fori_loop(1, PAIRS - 3, steps, 0, unroll=2)
-    step(PAIRS - 3)
-    step(PAIRS - 2, final=True)
-    step(PAIRS - 1, final=True)
+    for group, (low, high) in enumerate(GROUPS):
+        for move in moves(group):
+            move.wait()
+        if low == 0:
+            step(0, first=True)
+            tables[1].wait()
+            low = 1
+        if high - low > 1:
+            lax.fori_loop(low, high - (high - low) % 2, steps, 0, unroll=2)
+        if (high - low) % 2:
+            step(high - 1)
     forward(PAIRS - 1)
 
 
@@ -405,8 +421,8 @@
             pltpu.VMEM(inv.shape, BF),
             pltpu.VMEM(fwd.shape, BF),
             pltpu.VMEM((2, PLANE, ZP * BC), BF),
-            pltpu.SemaphoreType.DMA((PAIRS,)),
-            pltpu.SemaphoreType.DMA((PAIRS,)),
+            pltpu.SemaphoreType.DMA((len(GROUPS),)),
+            pltpu.SemaphoreType.DMA((len(GROUPS),)),
             pltpu.SemaphoreType.DMA((2,)),
         ],
         "middle",
@@ -415,11 +431,18 @@
     )(recv, far(x), far(cot), far(inv), far(fwd), mix, bias)
 
 
+def halves(source, target, sem):
+    cut = STEP_CELLS * NY
+    parts = [pl.ds(0, cut), pl.ds(cut, ZL * XL * NY - cut)]
+    return [
+        pltpu.make_async_copy(source.at[rows, :], target.at[rows, :], sem.at[k])
+        for k, rows in enumerate(parts)
+    ]
+
+
 def last_kernel(recv_ref, pre_ref, inv_ref, mix_ref, out_ref, in_ref, made_ref, wide_ref, in_sem, sem):
-    fetches = [
-        pltpu.make_async_copy(rows_of(pre_ref, i), in_ref.at[i], in_sem.at[i]) for i in range(STEPS)
-    ]
-    for copy in fetches[:2]:
+    fetches = halves(pre_ref, in_ref, in_sem)
+    for copy in fetches:
         copy.start()
     copies = []
     for i in range(STEPS):
@@ -427,11 +450,10 @@
             pair = 2 * i + j
             modes = split_pair(recv_ref[:, pair * ROWS : (pair + 1) * ROWS, :])
             cells = dot(modes, inv_ref[...], ((0,), (0,)))
-            if j == 0:
+            if j == 0 and i < len(fetches):
                 fetches[i].wait()
-                if i + 2 < STEPS:
-                    fetches[i + 2].start()
-            rows = in_ref[i, j * ZP * PLANE : (j + 1) * ZP * PLANE, :]
+            at = pair * ZP * PLANE
+            rows = in_ref[at : at + ZP * PLANE, :]
             local = dot(mix_ref[...], rows, ((1,), (1,)))
             for z in range(ZP):
                 for t in range(XL):
@@ -454,10 +476,10 @@
         [VMEM, REMOTE, VMEM, VMEM],
         REMOTE,
         [
-            pltpu.VMEM((STEPS, STEP_CELLS * NY, BC), BF),
+            pltpu.VMEM((ZL * XL * NY, BC), BF),
             pltpu.VMEM((STEPS, BC, STEP_CELLS, NY), BF),
             pltpu.VMEM((2, BC * STEP_CELLS, NY), F32),
-            pltpu.SemaphoreType.DMA((STEPS,)),
+            pltpu.SemaphoreType.DMA((2,)),
             pltpu.SemaphoreType.DMA((STEPS,)),
         ],
         "last",
@@ -503,7 +525,7 @@
         ]
     ).astype(BF)
     recv = exchange(z_inverse(mixed, t["z_inv"]), "gz")
-    recv = exchange(x_transform(recv, t["x_inv"], XY, INVERSE, "x_inverse"), "xy")
+    recv = exchange(x_transform(recv, t["x_inv"], XY, INVERSE, "x_inverse", True), "xy")
     cot_lanes = to_lanes(cot)
     send, layer, pre = middle(
         recv, x_lanes, cot_lanes, t["doubled_t"], t["doubled"], mix, bias
@@ -523,7 +545,7 @@
         "rkmbo,kmio->rkmbi", paired, weights, preferred_element_type=F32
     ).astype(BF)
     recv = exchange(z_inverse(spectra_grad, t["z_inv"]), "gz")
-    recv = exchange(x_transform(recv, t["x_inv"], XY, FORWARD, "x_inverse"), "xy")
+    recv = exchange(x_transform(recv, t["x_inv"], XY, FORWARD, "x_inverse", True), "xy")
     spectral_grad = jnp.einsum(
         "rkmbi,rkmbo->kmio", spectra, paired, preferred_element_type=F32
     ).astype(BF)

time: 207 us -> 204 us (0.986)
  Pallas kernels: 28.2 us -> 25.2 us
    pallas_call x1, Pallas kernels: 7.67 us -> 5.54 us  [middle(): call(middle_kernel, [jax.ShapeDtypeStruct((MY, PAIRS * ROWS, BC), BF), fl...]
where the time goes in v2:
time: 204 us; the launch traced here: 203 us
  blocking collectives  114 us (56%)
  waiting for transfers between devices  40.6 us (20%)
  Pallas kernels  25.2 us (12%)
  starting transfers between devices  11.2 us (5%)
  local copies, waits for them, and re-layouts  6.47 us (3%)
  matrix products  3.99 us (2%)
    all_to_all x6, blocking collectives, exchange(): return lax.all_to_all(x, axis, split_axis=0, concat_axis=0, tiled=True)  114 us
    all_to_all x2, waiting for transfers between devices, exchange(): return lax.all_to_all(x, axis, split_axis=0, concat_axis=0, tiled=True)  40.6 us
    all_to_all x2, starting transfers between devices, exchange(): return lax.all_to_all(x, axis, split_axis=0, concat_axis=0, tiled=True)  11.2 us
    pallas_call x2, Pallas kernels, to_lanes(): call(to_lanes_kernel, jax.ShapeDtypeStruct((ZL * XL * NY, BC), BF), [REMO...  5.81 us
    pallas_call x1, Pallas kernels, middle(): call(middle_kernel, [jax.ShapeDtypeStruct((MY, PAIRS * ROWS, BC), BF), fl...  5.54 us
  transfers between devices with their start and end apart: 2, of which 2 were waited for; matrix products, arithmetic and copies ran while one was open for 1% of the time, Pallas kernels for 5%

profile of v2, /device:TPU:2, one launch (start us, length us, event | category | flops | bytes accessed | tf_op | source)
XLA Modules:
  0.0 203.3 jit_solution(10031296581417701094)
XLA Ops:
  0.7 3.3 %y_first.1 = bf16[32,128,128]{2,1,0:T(8,128)(2,1)S(1)} custom-call(bf16[128,64,128]{2,1,0:T(8,128)(2,1)} %bitcast.56, bf16[256,512]{1,0:T(8,128)(2,1)} %constant.75.clone.far_ref.inv_ref), custom_call_target="tpu_custom_call" | custom-call | flops 536870912 | bytes 4194304 | tf_op jit(solution)/shard_map/y_first/pallas_call | solution.py:174
  3.9 39.6 %all_to_all.40.recv_ref = bf16[32,128,128]{2,1,0:T(8,128)(2,1)S(1)} all-to-all(bf16[32,128,128]{2,1,0:T(8,128)(2,1)S(1)} %y_first.1), channel_id=1, replica_groups=mesh['gz'=8,'xy'=32] {'xy'}, dimensions={0} | all-to-all | bytes 2097152 | tf_op jit(solution)/shard_map/all_to_all | solution.py:492
  43.6 0.3 x_forward.2
  43.9 11.8 %all_to_all.41 = bf16[8,128,128]{2,1,0:T(8,128)(2,1)S(1)} all-to-all(bf16[8,128,128]{2,1,0:T(8,128)(2,1)S(1)} %x_forward.2), channel_id=1, replica_groups=mesh['gz'=8,'xy'=32] {'gz'}, dimensions={0} | all-to-all | bytes 524288 | tf_op jit(solution)/shard_map/all_to_all | solution.py:492
  55.7 0.3 fusion.16
  56.0 0.1 copy.25
  56.1 0.1 reshape.123
  56.3 0.7 fusion.7
  56.9 0.3 fusion.19
  57.3 0.2 pad_maximum_fusion
  57.5 0.1 copy.27
  57.6 0.1 convert_element_type.40
  57.7 0.3 fusion.5
  58.1 0.2 copy.28
  58.2 9.9 %all_to_all.42.recv_ref = bf16[8,128,128]{2,1,0:T(8,128)(2,1)S(1)} all-to-all(bf16[8,128,128]{2,1,0:T(8,128)(2,1)S(1)} %bitcast.64), channel_id=1, replica_groups=mesh['gz'=8,'xy'=32] {'gz'}, dimensions={0} | all-to-all | bytes 524288 | tf_op jit(solution)/shard_map/all_to_all | solution.py:492
  68.2 1.3 x_inverse.2
  69.5 5.6 %all-to-all-start.3 = ((bf16[32,128,128]{2,1,0:T(8,128)(2,1)}), bf16[32,128,128]{2,1,0:T(8,128)(2,1)S(1)}, u32[]{:S(2)}, u32[]{:S(2)}) async-start(bf16[32,128,128]{2,1,0:T(8,128)(2,1)} %x_inverse.2), calls=%async_computation.3 | async-start | bytes 2097152 | tf_op jit(solution)/shard_map/all_to_all | solution.py:492
  75.1 2.9 %to_lanes.2.x_far = bf16[8192,128]{1,0:T(8,128)(2,1)S(1)} custom-call(bf16[128,64,128]{2,1,0:T(8,128)(2,1)} %bitcast.57), custom_call_target="tpu_custom_call" | custom-call | bytes 12582912 | tf_op jit(solution)/shard_map/to_lanes/pallas_call | solution.py:211
  78.0 1.3 copy-done.1
  79.3 0.1 broadcast_in_dim_tile.3.bias_ref
  79.5 0.1 reshape.127.mix_ref
  79.6 2.9 %to_lanes.3.cot_far = bf16[8192,128]{1,0:T(8,128)(2,1)S(1)} custom-call(bf16[128,64,128]{2,1,0:T(8,128)(2,1)} %bitcast.58), custom_call_target="tpu_custom_call" | custom-call | bytes 12582912 | tf_op jit(solution)/shard_map/to_lanes/pallas_call | solution.py:211
  82.5 1.3 copy-done.2
  83.8 18.9 %all-to-all-done.3.recv_ref = bf16[32,128,128]{2,1,0:T(8,128)(2,1)S(1)} async-done(((bf16[32,128,128]{2,1,0:T(8,128)(2,1)}), bf16[32,128,128]{2,1,0:T(8,128)(2,1)S(1)}, u32[]{:S(2)}, u32[]{:S(2)}) %all-to-all-start.3) | async-done | bytes 1048608 | tf_op jit(solution)/shard_map/all_to_all | solution.py:492
  102.7 5.5 %middle.1 = (bf16[32,128,128]{2,1,0:T(8,128)(2,1)S(1)}, bf16[8192,128]{1,0:T(8,128)(2,1)S(1)}, bf16[8192,128]{1,0:T(8,128)(2,1)S(1)}) custom-call(bf16[32,128,128]{2,1,0:T(8,128)(2,1)S(1)} %all-to-all-done.3.recv_ref, bf16[8192,128]{1,0:T(8,128)(2,1)} %copy-done.1, bf16[8192,128]{1,0:T(8,128)(2,1)} %copy-done.2, bf16[512,256]{1,0:T(8,128)(2,1)} %constant.77.clone.inv_far, ...), custom_call_target="tpu_custom_call" | custom-call | flops 1073741824 | bytes 12582912 | tf_op jit(solution)/shard_map/middle/pallas_call | solution.py:413
  108.3 32.2 %all_to_all.43.recv_ref = bf16[32,128,128]{2,1,0:T(8,128)(2,1)S(1)} all-to-all(bf16[32,128,128]{2,1,0:T(8,128)(2,1)S(1)} %get-tuple-element.31), channel_id=1, replica_groups=mesh['gz'=8,'xy'=32] {'xy'}, dimensions={0} | all-to-all | bytes 2097152 | tf_op jit(solution)/shard_map/all_to_all | solution.py:492
  140.6 0.3 x_forward.3
  140.9 10.0 %all_to_all.44 = bf16[8,128,128]{2,1,0:T(8,128)(2,1)S(1)} all-to-all(bf16[8,128,128]{2,1,0:T(8,128)(2,1)S(1)} %x_forward.3), channel_id=1, replica_groups=mesh['gz'=8,'xy'=32] {'gz'}, dimensions={0} | all-to-all | bytes 524288 | tf_op jit(solution)/shard_map/all_to_all | solution.py:492
  150.9 0.3 fusion.17
  151.2 0.1 copy.31
  151.4 0.1 squeeze.15
  151.5 0.1 copy.30
  151.6 0.1 squeeze.14
  151.8 0.4 maximum_bitcast_fusion
  152.1 0.6 copy-done.14
  152.7 1.2 fusion.13
  153.9 0.1 copy.32
  154.0 0.1 reshape.130
  154.2 0.3 fusion.6
  154.5 0.2 copy.33
  154.6 9.9 %all_to_all.45.recv_ref = bf16[8,128,128]{2,1,0:T(8,128)(2,1)S(1)} all-to-all(bf16[8,128,128]{2,1,0:T(8,128)(2,1)S(1)} %bitcast.65), channel_id=1, replica_groups=mesh['gz'=8,'xy'=32] {'gz'}, dimensions={0} | all-to-all | bytes 524288 | tf_op jit(solution)/shard_map/all_to_all | solution.py:492
  164.6 1.3 x_inverse.3
  165.9 5.6 %all-to-all-start.7 = ((bf16[32,128,128]{2,1,0:T(8,128)(2,1)}), bf16[32,128,128]{2,1,0:T(8,128)(2,1)S(1)}, u32[]{:S(2)}, u32[]{:S(2)}) async-start(bf16[32,128,128]{2,1,0:T(8,128)(2,1)} %x_inverse.3), calls=%async_computation.7 | async-start | bytes 2097152 | tf_op jit(solution)/shard_map/all_to_all | solution.py:492
  171.5 3.5 %from_lanes.1 = bf16[128,64,128]{2,1,0:T(8,128)(2,1)} custom-call(bf16[8192,128]{1,0:T(8,128)(2,1)} %copy-done.4), custom_call_target="tpu_custom_call" | custom-call | bytes 12582912 | tf_op jit(solution)/shard_map/from_lanes/pallas_call | solution.py:249
  175.0 0.9 fusion.20
  175.9 1.5 copy.51
  177.4 21.7 %all-to-all-done.7.recv_ref = bf16[32,128,128]{2,1,0:T(8,128)(2,1)S(1)} async-done(((bf16[32,128,128]{2,1,0:T(8,128)(2,1)}), bf16[32,128,128]{2,1,0:T(8,128)(2,1)S(1)}, u32[]{:S(2)}, u32[]{:S(2)}) %all-to-all-start.7) | async-done | bytes 1048608 | tf_op jit(solution)/shard_map/all_to_all | solution.py:492
  199.2 3.9 %last.1 = bf16[128,64,128]{2,1,0:T(8,128)(2,1)} custom-call(bf16[32,128,128]{2,1,0:T(8,128)(2,1)S(1)} %all-to-all-done.7.recv_ref, bf16[8192,128]{1,0:T(8,128)(2,1)} %copy-done.3, bf16[256,512]{1,0:T(8,128)(2,1)S(1)} %copy-done.5, bf16[128,128]{1,0:T(8,128)(2,1)S(1)} %reshape.127.mix_ref), custom_call_target="tpu_custom_call" | custom-call | flops 1073741824 | bytes 8388608 | tf_op jit(solution)/shard_map/last/pallas_call | solution.py:473
  (39 shorter events, 0.3 us)
Async XLA Ops:
  0.6 55.6 %copy-start = (bf16[1,4,32,64,128]{4,3,2,1,0:T(8,128)(2,1)S(1)}, bf16[1,4,32,64,128]{4,3,2,1,0:T(8,128)(2,1)}, u32[]{:S(2)}) copy-start(bf16[1,4,32,64,128]{4,3,2,1,0:T(8,128)(2,1)} %param.18) | copy-start | bytes 6291460
  0.6 42.9 %copy-start.7 = (bf16[128,512]{1,0:T(8,128)(2,1)S(1)}, bf16[128,512]{1,0:T(8,128)(2,1)}, u32[]{:S(2)}) copy-start(bf16[128,512]{1,0:T(8,128)(2,1)} %constant.78.clone.table_ref) | copy-start | bytes 393220
  3.9 51.8 %copy-start.10 = (bf16[256,1024]{1,0:T(8,128)(2,1)S(1)}, bf16[256,1024]{1,0:T(8,128)(2,1)}, u32[]{:S(2)}) copy-start(bf16[256,1024]{1,0:T(8,128)(2,1)} %constant.80.clone) | copy-start | bytes 1572868
  56.0 1.7 copy-start.8
  56.3 1.8 copy-start.12
  56.9 11.3 %copy-start.6 = (bf16[512,128]{1,0:T(8,128)(2,1)S(1)}, bf16[512,128]{1,0:T(8,128)(2,1)}, u32[]{:S(2)}) copy-start(bf16[512,128]{1,0:T(8,128)(2,1)} %constant.79.clone.table_ref) | copy-start | bytes 393220
  69.5 33.3 %all-to-all-start.3 = ((bf16[32,128,128]{2,1,0:T(8,128)(2,1)}), bf16[32,128,128]{2,1,0:T(8,128)(2,1)S(1)}, u32[]{:S(2)}, u32[]{:S(2)}) async-start(bf16[32,128,128]{2,1,0:T(8,128)(2,1)} %x_inverse.2), calls=%async_computation.3 | async-start | bytes 2097152 | tf_op jit(solution)/shard_map/all_to_all | solution.py:492
  75.1 4.3 %copy-start.17 = (f32[64]{0:T(128)S(1)}, f32[64]{0:T(128)}, u32[]{:S(2)}) copy-start(f32[64]{0:T(128)} %param.20) | copy-start | bytes 772
  75.1 4.3 %copy-start.16 = (bf16[64,64]{1,0:T(8,128)(2,1)S(1)}, bf16[64,64]{1,0:T(8,128)(2,1)}, u32[]{:S(2)}) copy-start(bf16[64,64]{1,0:T(8,128)(2,1)} %param.19) | copy-start | bytes 24580
  78.0 1.3 copy-start.1
  82.5 1.3 copy-start.2
  108.3 42.9 %copy-start.3 = (bf16[8192,128]{1,0:T(8,128)(2,1)}, bf16[8192,128]{1,0:T(8,128)(2,1)S(1)}, u32[]{:S(2)}) copy-start(bf16[8192,128]{1,0:T(8,128)(2,1)S(1)} %get-tuple-element.32.pre_ref) | copy-start | bytes 6291460
  108.3 42.9 %copy-start.4 = (bf16[8192,128]{1,0:T(8,128)(2,1)}, bf16[8192,128]{1,0:T(8,128)(2,1)S(1)}, u32[]{:S(2)}) copy-start(bf16[8192,128]{1,0:T(8,128)(2,1)S(1)} %get-tuple-element.30.x_ref) | copy-start | bytes 6291460
  108.3 42.6 %copy-start.11 = (bf16[256,1024]{1,0:T(8,128)(2,1)S(1)}, bf16[256,1024]{1,0:T(8,128)(2,1)}, u32[]{:S(2)}) copy-start(bf16[256,1024]{1,0:T(8,128)(2,1)} %constant.80.clone) | copy-start | bytes 1572868
  150.9 3.3 %copy-start.9 = (bf16[1024,256]{1,0:T(8,128)(2,1)S(1)}, bf16[1024,256]{1,0:T(8,128)(2,1)}, u32[]{:S(2)}) copy-start(bf16[1024,256]{1,0:T(8,128)(2,1)} %constant.81.clone) | copy-start | bytes 1572868
  152.1 0.6 copy-start.14
  165.9 33.3 %all-to-all-start.7 = ((bf16[32,128,128]{2,1,0:T(8,128)(2,1)}), bf16[32,128,128]{2,1,0:T(8,128)(2,1)S(1)}, u32[]{:S(2)}, u32[]{:S(2)}) async-start(bf16[32,128,128]{2,1,0:T(8,128)(2,1)} %x_inverse.3), calls=%async_computation.7 | async-start | bytes 2097152 | tf_op jit(solution)/shard_map/all_to_all | solution.py:492
  171.5 3.5 %copy-start.13 = (bf16[2,4,32,2,64]{4,3,2,1,0:T(2,128)(2,1)S(1)}, bf16[2,4,32,2,64]{4,3,2,1,0:T(2,128)(2,1)}, u32[]{:S(2)}) copy-start(bf16[2,4,32,2,64]{4,3,2,1,0:T(2,128)(2,1)} %copy-done.12) | copy-start | bytes 196612
  171.5 3.5 %copy-start.15 = (bf16[1,4,32,2,128]{4,3,0,2,1:T(2,128)(2,1)S(1)}, bf16[1,4,32,2,128]{4,3,0,2,1:T(2,128)(2,1)}, u32[]{:S(2)}) copy-start(bf16[1,4,32,2,128]{4,3,0,2,1:T(2,128)(2,1)} %copy-done.14) | copy-start | bytes 196612
  175.9 23.2 %copy-start.5 = (bf16[256,512]{1,0:T(8,128)(2,1)S(1)}, bf16[256,512]{1,0:T(8,128)(2,1)}, u32[]{:S(2)}) copy-start(bf16[256,512]{1,0:T(8,128)(2,1)} %constant.75.clone.far_ref.inv_ref) | copy-start | bytes 786436

commit v3 on v2

--- a/solution.py
+++ b/solution.py
@@ -495,13 +495,45 @@
 KX = MX // GZ
 
 
+def z_forward_kernel(recv_ref, table_ref, real_ref, imag_ref):
+    half = KX * MZ
+    rows = recv_ref[...].reshape(GZ * PAIRS * ROWS, BC)
+    real_ref[...] = dot(table_ref[:half, :], rows).astype(BF)
+    imag_ref[...] = dot(table_ref[half:, :], rows).astype(BF)
+
+
 def z_forward(recv, table):
-    modes = dot(table, recv.reshape(GZ * PAIRS * ROWS, BC))
-    return modes.astype(BF).reshape(2, KX, MZ, BATCH, C)
-
-
-def z_inverse(modes, table):
-    return dot(table, modes.reshape(2 * KX * MZ, BC)).astype(BF).reshape(GZ, PAIRS * ROWS, BC)
+    part = jax.ShapeDtypeStruct((KX * MZ, BC), BF)
+    parts = call(
+        z_forward_kernel,
+        [part, part],
+        [VMEM] * 2,
+        [VMEM] * 2,
+        [],
+        "z_forward",
+        1 << 26,
+        1 << 20,
+    )(recv, table)
+    return [x.reshape(KX, MZ, BATCH, C) for x in parts]
+
+
+def z_inverse_kernel(real_ref, imag_ref, table_ref, out_ref):
+    half = KX * MZ
+    total = dot(table_ref[:, :half], real_ref[...]) + dot(table_ref[:, half:], imag_ref[...])
+    out_ref[...] = total.astype(BF).reshape(GZ, PAIRS * ROWS, BC)
+
+
+def z_inverse(real, imag, table):
+    return call(
+        z_inverse_kernel,
+        jax.ShapeDtypeStruct((GZ, PAIRS * ROWS, BC), BF),
+        [VMEM] * 3,
+        VMEM,
+        [],
+        "z_inverse",
+        1 << 26,
+        1 << 20,
+    )(real.reshape(KX * MZ, BC), imag.reshape(KX * MZ, BC), table)
 
 
 def body(features, cotangent, spectral, pointwise, channel_bias):
@@ -516,15 +548,11 @@
     recv = exchange(y_first(x, t["unit"]), "xy")
     x_lanes = to_lanes(x)
     recv = exchange(x_transform(recv, t["x_fwd"], GZ, FORWARD, "x_forward"), "gz")
-    spectra = z_forward(recv, t["z_fwd"])
+    spectra = jnp.stack(z_forward(recv, t["z_fwd"]))
     products = jnp.einsum("rkmbi,kmio->rkmbo", spectra, weights, preferred_element_type=F32)
-    mixed = jnp.stack(
-        [
-            products[0, ..., :C] - products[1, ..., C:],
-            products[0, ..., C:] + products[1, ..., :C],
-        ]
-    ).astype(BF)
-    recv = exchange(z_inverse(mixed, t["z_inv"]), "gz")
+    real = (products[0, ..., :C] - products[1, ..., C:]).astype(BF)
+    imag = (products[0, ..., C:] + products[1, ..., :C]).astype(BF)
+    recv = exchange(z_inverse(real, imag, t["z_inv"]), "gz")
     recv = exchange(x_transform(recv, t["x_inv"], XY, INVERSE, "x_inverse", True), "xy")
     cot_lanes = to_lanes(cot)
     send, layer, pre = middle(
@@ -533,8 +561,7 @@
     recv = exchange(send, "xy")
     layer_out = from_lanes(layer)
     recv = exchange(x_transform(recv, t["x_fwd"], GZ, INVERSE, "x_forward"), "gz")
-    mode_grad = z_forward(recv, t["z_fwd"])
-    real, imag = mode_grad[0], mode_grad[1]
+    real, imag = z_forward(recv, t["z_fwd"])
     paired = jnp.stack(
         [
             jnp.concatenate([real, imag], axis=-1),
@@ -544,7 +571,7 @@
     spectra_grad = jnp.einsum(
         "rkmbo,kmio->rkmbi", paired, weights, preferred_element_type=F32
     ).astype(BF)
-    recv = exchange(z_inverse(spectra_grad, t["z_inv"]), "gz")
+    recv = exchange(z_inverse(spectra_grad[0], spectra_grad[1], t["z_inv"]), "gz")
     recv = exchange(x_transform(recv, t["x_inv"], XY, FORWARD, "x_inverse", True), "xy")
     spectral_grad = jnp.einsum(
         "rkmbi,rkmbo->kmio", spectra, paired, preferred_element_type=F32

time: 204 us -> 202 us (level)
  local copies, waits for them, and re-layouts: 6.47 us -> 3.84 us
where the time goes in v3:
time: 202 us
  blocking collectives  114 us (56%)
  waiting for transfers between devices  40.8 us (20%)
  Pallas kernels  26.3 us (13%)
  starting transfers between devices  11.1 us (5%)
  matrix products  4.08 us (2%)
  local copies, waits for them, and re-layouts  3.84 us (2%)
    all_to_all x6, blocking collectives, exchange(): return lax.all_to_all(x, axis, split_axis=0, concat_axis=0, tiled=True)  114 us
    all_to_all x2, waiting for transfers between devices, exchange(): return lax.all_to_all(x, axis, split_axis=0, concat_axis=0, tiled=True)  40.8 us
    all_to_all x2, starting transfers between devices, exchange(): return lax.all_to_all(x, axis, split_axis=0, concat_axis=0, tiled=True)  11.1 us
    pallas_call x2, Pallas kernels, to_lanes(): call(to_lanes_kernel, jax.ShapeDtypeStruct((ZL * XL * NY, BC), BF), [REMO...  5.81 us
    pallas_call x1, Pallas kernels, middle(): call(middle_kernel, [jax.ShapeDtypeStruct((MY, PAIRS * ROWS, BC), BF), fl...  5.53 us
  transfers between devices with their start and end apart: 2, of which 2 were waited for; matrix products, arithmetic and copies ran while one was open for 1% of the time, Pallas kernels for 5%

profile of v3, /device:TPU:2, one launch (start us, length us, event | category | flops | bytes accessed | tf_op | source)
XLA Modules:
  0.0 201.7 jit_solution(3137079260047608777)
XLA Ops:
  0.6 0.0 copy-start
  0.6 0.0 copy-start.11
  0.7 3.3 %y_first.1 = bf16[32,128,128]{2,1,0:T(8,128)(2,1)S(1)} custom-call(bf16[128,64,128]{2,1,0:T(8,128)(2,1)} %bitcast.47, bf16[256,512]{1,0:T(8,128)(2,1)} %constant.75.clone.far_ref.inv_ref), custom_call_target="tpu_custom_call" | custom-call | flops 536870912 | bytes 4194304 | tf_op jit(solution)/shard_map/y_first/pallas_call | solution.py:174
  3.9 0.0 copy-start.3
  3.9 39.6 %all_to_all.40.recv_ref = bf16[32,128,128]{2,1,0:T(8,128)(2,1)S(1)} all-to-all(bf16[32,128,128]{2,1,0:T(8,128)(2,1)S(1)} %y_first.1), channel_id=1, replica_groups=mesh['gz'=8,'xy'=32] {'xy'}, dimensions={0} | all-to-all | bytes 2097152 | tf_op jit(solution)/shard_map/all_to_all | solution.py:492
  43.6 0.3 x_forward.2
  43.9 11.8 %all_to_all.41.recv_ref = bf16[8,128,128]{2,1,0:T(8,128)(2,1)S(1)} all-to-all(bf16[8,128,128]{2,1,0:T(8,128)(2,1)S(1)} %x_forward.2), channel_id=1, replica_groups=mesh['gz'=8,'xy'=32] {'gz'}, dimensions={0} | all-to-all | bytes 524288 | tf_op jit(solution)/shard_map/all_to_all | solution.py:492
  55.7 0.3 z_forward.2
  56.0 0.1 stack_reshape.6
  56.1 0.1 stack_reshape.7
  56.2 0.0 copy-start.10
  56.2 0.7 fusion.5
  56.9 0.3 fusion.14
  57.2 0.1 convert_element_type.26.imag_ref
  57.3 0.1 convert_element_type.24.real_ref
  57.4 0.3 z_inverse.2
  57.7 9.9 %all_to_all.42.recv_ref = bf16[8,128,128]{2,1,0:T(8,128)(2,1)S(1)} all-to-all(bf16[8,128,128]{2,1,0:T(8,128)(2,1)S(1)} %z_inverse.2), channel_id=1, replica_groups=mesh['gz'=8,'xy'=32] {'gz'}, dimensions={0} | all-to-all | bytes 524288 | tf_op jit(solution)/shard_map/all_to_all | solution.py:492
  67.7 1.3 x_inverse.2
  69.0 5.6 %all-to-all-start.3 = ((bf16[32,128,128]{2,1,0:T(8,128)(2,1)}), bf16[32,128,128]{2,1,0:T(8,128)(2,1)S(1)}, u32[]{:S(2)}, u32[]{:S(2)}) async-start(bf16[32,128,128]{2,1,0:T(8,128)(2,1)} %x_inverse.2), calls=%async_computation.3 | async-start | bytes 2097152 | tf_op jit(solution)/shard_map/all_to_all | solution.py:492
  74.6 2.9 %to_lanes.2.x_far = bf16[8192,128]{1,0:T(8,128)(2,1)S(1)} custom-call(bf16[128,64,128]{2,1,0:T(8,128)(2,1)} %bitcast.48), custom_call_target="tpu_custom_call" | custom-call | bytes 12582912 | tf_op jit(solution)/shard_map/to_lanes/pallas_call | solution.py:211
  77.5 1.3 copy-done.1
  78.8 0.1 broadcast_in_dim_tile.3.bias_ref
  78.9 0.1 copy.17
  79.0 0.1 reshape.114.mix_ref
  79.1 2.9 %to_lanes.3.cot_far = bf16[8192,128]{1,0:T(8,128)(2,1)S(1)} custom-call(bf16[128,64,128]{2,1,0:T(8,128)(2,1)} %bitcast.49), custom_call_target="tpu_custom_call" | custom-call | bytes 12582912 | tf_op jit(solution)/shard_map/to_lanes/pallas_call | solution.py:211
  82.0 1.3 copy-done.2
  83.3 18.9 %all-to-all-done.3.recv_ref = bf16[32,128,128]{2,1,0:T(8,128)(2,1)S(1)} async-done(((bf16[32,128,128]{2,1,0:T(8,128)(2,1)}), bf16[32,128,128]{2,1,0:T(8,128)(2,1)S(1)}, u32[]{:S(2)}, u32[]{:S(2)}) %all-to-all-start.3) | async-done | bytes 1048608 | tf_op jit(solution)/shard_map/all_to_all | solution.py:492
  102.2 5.5 %middle.1 = (bf16[32,128,128]{2,1,0:T(8,128)(2,1)S(1)}, bf16[8192,128]{1,0:T(8,128)(2,1)S(1)}, bf16[8192,128]{1,0:T(8,128)(2,1)S(1)}) custom-call(bf16[32,128,128]{2,1,0:T(8,128)(2,1)S(1)} %all-to-all-done.3.recv_ref, bf16[8192,128]{1,0:T(8,128)(2,1)} %copy-done.1, bf16[8192,128]{1,0:T(8,128)(2,1)} %copy-done.2, bf16[512,256]{1,0:T(8,128)(2,1)} %constant.77.clone.inv_far, ...), custom_call_target="tpu_custom_call" | custom-call | flops 1073741824 | bytes 12582912 | tf_op jit(solution)/shard_map/middle/pallas_call | solution.py:413
  107.8 32.2 %all_to_all.43.recv_ref = bf16[32,128,128]{2,1,0:T(8,128)(2,1)S(1)} all-to-all(bf16[32,128,128]{2,1,0:T(8,128)(2,1)S(1)} %get-tuple-element.37), channel_id=1, replica_groups=mesh['gz'=8,'xy'=32] {'xy'}, dimensions={0} | all-to-all | bytes 2097152 | tf_op jit(solution)/shard_map/all_to_all | solution.py:492
  140.0 0.3 x_forward.3
  140.4 10.0 %all_to_all.44.recv_ref = bf16[8,128,128]{2,1,0:T(8,128)(2,1)S(1)} all-to-all(bf16[8,128,128]{2,1,0:T(8,128)(2,1)S(1)} %x_forward.3), channel_id=1, replica_groups=mesh['gz'=8,'xy'=32] {'gz'}, dimensions={0} | all-to-all | bytes 524288 | tf_op jit(solution)/shard_map/all_to_all | solution.py:492
  150.4 0.3 z_forward.3
  150.7 0.1 reshape.116
  150.8 0.1 neg.3
  150.8 0.1 reshape.117
  150.9 0.4 maximum_bitcast_fusion
  151.3 1.2 fusion.11
  152.5 0.1 fusion.16
  152.6 0.1 reshape_squeeze.7.imag_ref
  152.7 0.1 reshape_squeeze.6.real_ref
  152.8 0.3 z_inverse.3
  153.1 9.9 %all_to_all.45.recv_ref = bf16[8,128,128]{2,1,0:T(8,128)(2,1)S(1)} all-to-all(bf16[8,128,128]{2,1,0:T(8,128)(2,1)S(1)} %z_inverse.3), channel_id=1, replica_groups=mesh['gz'=8,'xy'=32] {'gz'}, dimensions={0} | all-to-all | bytes 524288 | tf_op jit(solution)/shard_map/all_to_all | solution.py:492
  163.1 1.3 x_inverse.3
  164.3 5.6 %all-to-all-start.7 = ((bf16[32,128,128]{2,1,0:T(8,128)(2,1)}), bf16[32,128,128]{2,1,0:T(8,128)(2,1)S(1)}, u32[]{:S(2)}, u32[]{:S(2)}) async-start(bf16[32,128,128]{2,1,0:T(8,128)(2,1)} %x_inverse.3), calls=%async_computation.7 | async-start | bytes 2097152 | tf_op jit(solution)/shard_map/all_to_all | solution.py:492
  169.9 3.5 %from_lanes.1 = bf16[128,64,128]{2,1,0:T(8,128)(2,1)} custom-call(bf16[8192,128]{1,0:T(8,128)(2,1)} %copy-done.6), custom_call_target="tpu_custom_call" | custom-call | bytes 12582912 | tf_op jit(solution)/shard_map/from_lanes/pallas_call | solution.py:249
  173.5 2.2 %fusion.4 = bf16[1,4,32,64,128]{4,3,2,1,0:T(8,128)(2,1)} fusion(bf16[1,4,32,2,128]{4,3,0,2,1:T(2,128)(2,1)S(1)} %copy-done.13, bf16[1,4,32,2,128]{4,3,0,2,1:T(2,128)(2,1)S(1)} %get-tuple-element.45, bf16[1,4,32,2,64]{4,3,0,2,1:T(2,128)(2,1)S(1)} %bitcast.55, bf16[1,4,32,2,64]{4,3,0,2,1:T(2,128)(2,1)S(1)} %bitcast.53), kind=kOutput, calls=%fused_computation.5 | convolution fusion | flops 9830400 | bytes 2293760 | tf_op jit(solution)/shard_map/rkmbi,rkmbo->kmio/dot_general | solution.py:576
  175.7 21.9 %all-to-all-done.7.recv_ref = bf16[32,128,128]{2,1,0:T(8,128)(2,1)S(1)} async-done(((bf16[32,128,128]{2,1,0:T(8,128)(2,1)}), bf16[32,128,128]{2,1,0:T(8,128)(2,1)S(1)}, u32[]{:S(2)}, u32[]{:S(2)}) %all-to-all-start.7) | async-done | bytes 1048608 | tf_op jit(solution)/shard_map/all_to_all | solution.py:492
  197.6 3.9 %last.1 = bf16[128,64,128]{2,1,0:T(8,128)(2,1)} custom-call(bf16[32,128,128]{2,1,0:T(8,128)(2,1)S(1)} %all-to-all-done.7.recv_ref, bf16[8192,128]{1,0:T(8,128)(2,1)} %copy-done.5, bf16[256,512]{1,0:T(8,128)(2,1)S(1)} %copy-done.9, bf16[128,128]{1,0:T(8,128)(2,1)S(1)} %reshape.114.mix_ref), custom_call_target="tpu_custom_call" | custom-call | flops 1073741824 | bytes 8388608 | tf_op jit(solution)/shard_map/last/pallas_call | solution.py:473
  (37 shorter events, 0.1 us)
Async XLA Ops:
  0.6 55.6 %copy-start = (bf16[1,4,32,64,128]{4,3,2,1,0:T(8,128)(2,1)S(1)}, bf16[1,4,32,64,128]{4,3,2,1,0:T(8,128)(2,1)}, u32[]{:S(2)}) copy-start(bf16[1,4,32,64,128]{4,3,2,1,0:T(8,128)(2,1)} %param.18) | copy-start | bytes 6291460
  0.6 42.9 %copy-start.11 = (bf16[128,512]{1,0:T(8,128)(2,1)S(1)}, bf16[128,512]{1,0:T(8,128)(2,1)}, u32[]{:S(2)}) copy-start(bf16[128,512]{1,0:T(8,128)(2,1)} %constant.78.clone.table_ref) | copy-start | bytes 393220
  3.9 51.8 %copy-start.3 = (bf16[256,1024]{1,0:T(8,128)(2,1)S(1)}, bf16[256,1024]{1,0:T(8,128)(2,1)}, u32[]{:S(2)}) copy-start(bf16[256,1024]{1,0:T(8,128)(2,1)} %constant.80.clone.table_ref) | copy-start | bytes 1572868
  55.7 1.7 copy-start.7
  56.1 1.6 copy-start.14
  56.2 1.6 copy-start.16
  56.2 11.5 %copy-start.10 = (bf16[512,128]{1,0:T(8,128)(2,1)S(1)}, bf16[512,128]{1,0:T(8,128)(2,1)}, u32[]{:S(2)}) copy-start(bf16[512,128]{1,0:T(8,128)(2,1)} %constant.79.clone.table_ref) | copy-start | bytes 393220
  69.0 33.3 %all-to-all-start.3 = ((bf16[32,128,128]{2,1,0:T(8,128)(2,1)}), bf16[32,128,128]{2,1,0:T(8,128)(2,1)S(1)}, u32[]{:S(2)}, u32[]{:S(2)}) async-start(bf16[32,128,128]{2,1,0:T(8,128)(2,1)} %x_inverse.2), calls=%async_computation.3 | async-start | bytes 2097152 | tf_op jit(solution)/shard_map/all_to_all | solution.py:492
  74.5 4.3 %copy-start.19 = (f32[64]{0:T(128)S(1)}, f32[64]{0:T(128)}, u32[]{:S(2)}) copy-start(f32[64]{0:T(128)} %param.20) | copy-start | bytes 772
  74.6 4.3 %copy-start.18 = (bf16[64,64]{1,0:T(8,128)(2,1)S(1)}, bf16[64,64]{1,0:T(8,128)(2,1)}, u32[]{:S(2)}) copy-start(bf16[64,64]{1,0:T(8,128)(2,1)} %param.19) | copy-start | bytes 24580
  77.5 1.3 copy-start.1
  82.0 1.3 copy-start.2
  107.8 42.9 %copy-start.5 = (bf16[8192,128]{1,0:T(8,128)(2,1)}, bf16[8192,128]{1,0:T(8,128)(2,1)S(1)}, u32[]{:S(2)}) copy-start(bf16[8192,128]{1,0:T(8,128)(2,1)S(1)} %get-tuple-element.40.pre_ref) | copy-start | bytes 6291460
  107.8 42.9 %copy-start.6 = (bf16[8192,128]{1,0:T(8,128)(2,1)}, bf16[8192,128]{1,0:T(8,128)(2,1)S(1)}, u32[]{:S(2)}) copy-start(bf16[8192,128]{1,0:T(8,128)(2,1)S(1)} %get-tuple-element.36.x_ref) | copy-start | bytes 6291460
  107.8 42.6 %copy-start.4 = (bf16[256,1024]{1,0:T(8,128)(2,1)S(1)}, bf16[256,1024]{1,0:T(8,128)(2,1)}, u32[]{:S(2)}) copy-start(bf16[256,1024]{1,0:T(8,128)(2,1)} %constant.80.clone.table_ref) | copy-start | bytes 1572868
  150.4 2.4 %copy-start.8 = (bf16[1024,256]{1,0:T(8,128)(2,1)S(1)}, bf16[1024,256]{1,0:T(8,128)(2,1)}, u32[]{:S(2)}) copy-start(bf16[1024,256]{1,0:T(8,128)(2,1)} %constant.81.clone.table_ref) | copy-start | bytes 1572868
  151.3 11.8 %copy-start.12 = (bf16[1,4,32,2,128]{4,3,0,2,1:T(2,128)(2,1)}, bf16[1,4,32,2,128]{4,3,0,2,1:T(2,128)(2,1)S(1)}, u32[]{:S(2)}) copy-start(bf16[1,4,32,2,128]{4,3,0,2,1:T(2,128)(2,1)S(1)} %get-tuple-element.46) | copy-start | bytes 196612
  164.3 33.3 %all-to-all-start.7 = ((bf16[32,128,128]{2,1,0:T(8,128)(2,1)}), bf16[32,128,128]{2,1,0:T(8,128)(2,1)S(1)}, u32[]{:S(2)}, u32[]{:S(2)}) async-start(bf16[32,128,128]{2,1,0:T(8,128)(2,1)} %x_inverse.3), calls=%async_computation.7 | async-start | bytes 2097152 | tf_op jit(solution)/shard_map/all_to_all | solution.py:492
  169.9 3.6 %copy-start.13 = (bf16[1,4,32,2,128]{4,3,0,2,1:T(2,128)(2,1)S(1)}, bf16[1,4,32,2,128]{4,3,0,2,1:T(2,128)(2,1)}, u32[]{:S(2)}) copy-start(bf16[1,4,32,2,128]{4,3,0,2,1:T(2,128)(2,1)} %copy-done.12) | copy-start | bytes 196612
  169.9 3.6 %copy-start.15 = (bf16[1,4,32,2,64]{4,3,2,1,0:T(2,128)(2,1)S(1)}, bf16[1,4,32,2,64]{4,3,2,1,0:T(2,128)(2,1)}, u32[]{:S(2)}) copy-start(bf16[1,4,32,2,64]{4,3,2,1,0:T(2,128)(2,1)} %copy-done.14) | copy-start | bytes 98308
  169.9 3.6 %copy-start.17 = (bf16[1,4,32,2,64]{4,3,2,1,0:T(2,128)(2,1)S(1)}, bf16[1,4,32,2,64]{4,3,2,1,0:T(2,128)(2,1)}, u32[]{:S(2)}) copy-start(bf16[1,4,32,2,64]{4,3,2,1,0:T(2,128)(2,1)} %copy-done.16) | copy-start | bytes 98308
  173.5 24.1 %copy-start.9 = (bf16[256,512]{1,0:T(8,128)(2,1)S(1)}, bf16[256,512]{1,0:T(8,128)(2,1)}, u32[]{:S(2)}) copy-start(bf16[256,512]{1,0:T(8,128)(2,1)} %constant.75.clone.far_ref.inv_ref) | copy-start | bytes 786436

commit v4 on v3

--- a/solution.py
+++ b/solution.py
@@ -346,7 +346,7 @@
     ]
 
     tables[0].start()
-    for group in range(len(GROUPS)):
+    for group in range(2):
         for move in moves(group):
             move.start()
         if group == 0:
@@ -396,6 +396,9 @@
     for group, (low, high) in enumerate(GROUPS):
         for move in moves(group):
             move.wait()
+        if group + 2 < len(GROUPS):
+            for move in moves(group + 2):
+                move.start()
         if low == 0:
             step(0, first=True)
             tables[1].wait()

time: 202 us -> 203 us (level)
  no operation moved by 1% of the time
where the time goes in v4:
time: 203 us; the launch traced here: 202 us
  blocking collectives  114 us (56%)
  waiting for transfers between devices  40.8 us (20%)
  Pallas kernels  26.6 us (13%)
  starting transfers between devices  11.1 us (5%)
  matrix products  4.08 us (2%)
  local copies, waits for them, and re-layouts  3.84 us (2%)
    all_to_all x6, blocking collectives, exchange(): return lax.all_to_all(x, axis, split_axis=0, concat_axis=0, tiled=True)  114 us
    all_to_all x2, waiting for transfers between devices, exchange(): return lax.all_to_all(x, axis, split_axis=0, concat_axis=0, tiled=True)  40.8 us
    all_to_all x2, starting transfers between devices, exchange(): return lax.all_to_all(x, axis, split_axis=0, concat_axis=0, tiled=True)  11.1 us
    pallas_call x1, Pallas kernels, middle(): call(middle_kernel, [jax.ShapeDtypeStruct((MY, PAIRS * ROWS, BC), BF), fl...  5.82 us
    pallas_call x2, Pallas kernels, to_lanes(): call(to_lanes_kernel, jax.ShapeDtypeStruct((ZL * XL * NY, BC), BF), [REMO...  5.81 us
  transfers between devices with their start and end apart: 2, of which 2 were waited for; matrix products, arithmetic and copies ran while one was open for 1% of the time, Pallas kernels for 5%

profile of v4, /device:TPU:2, one launch (start us, length us, event | category | flops | bytes accessed | tf_op | source)
XLA Modules:
  0.0 202.0 jit_solution(1920897146183734677)
XLA Ops:
  0.6 0.0 copy-start
  0.6 0.0 copy-start.11
  0.7 3.3 %y_first.1 = bf16[32,128,128]{2,1,0:T(8,128)(2,1)S(1)} custom-call(bf16[128,64,128]{2,1,0:T(8,128)(2,1)} %bitcast.47, bf16[256,512]{1,0:T(8,128)(2,1)} %constant.75.clone.far_ref.inv_ref), custom_call_target="tpu_custom_call" | custom-call | flops 536870912 | bytes 4194304 | tf_op jit(solution)/shard_map/y_first/pallas_call | solution.py:174
  3.9 0.0 copy-start.3
  3.9 39.6 %all_to_all.40.recv_ref = bf16[32,128,128]{2,1,0:T(8,128)(2,1)S(1)} all-to-all(bf16[32,128,128]{2,1,0:T(8,128)(2,1)S(1)} %y_first.1), channel_id=1, replica_groups=mesh['gz'=8,'xy'=32] {'xy'}, dimensions={0} | all-to-all | bytes 2097152 | tf_op jit(solution)/shard_map/all_to_all | solution.py:495
  43.6 0.3 x_forward.2
  43.9 11.8 %all_to_all.41.recv_ref = bf16[8,128,128]{2,1,0:T(8,128)(2,1)S(1)} all-to-all(bf16[8,128,128]{2,1,0:T(8,128)(2,1)S(1)} %x_forward.2), channel_id=1, replica_groups=mesh['gz'=8,'xy'=32] {'gz'}, dimensions={0} | all-to-all | bytes 524288 | tf_op jit(solution)/shard_map/all_to_all | solution.py:495
  55.7 0.3 z_forward.2
  56.0 0.1 stack_reshape.6
  56.1 0.1 stack_reshape.7
  56.2 0.0 copy-start.10
  56.2 0.7 fusion.5
  56.9 0.3 fusion.14
  57.2 0.1 convert_element_type.26.imag_ref
  57.3 0.1 convert_element_type.24.real_ref
  57.4 0.3 z_inverse.2
  57.7 9.9 %all_to_all.42.recv_ref = bf16[8,128,128]{2,1,0:T(8,128)(2,1)S(1)} all-to-all(bf16[8,128,128]{2,1,0:T(8,128)(2,1)S(1)} %z_inverse.2), channel_id=1, replica_groups=mesh['gz'=8,'xy'=32] {'gz'}, dimensions={0} | all-to-all | bytes 524288 | tf_op jit(solution)/shard_map/all_to_all | solution.py:495
  67.7 1.3 x_inverse.2
  69.0 5.6 %all-to-all-start.3 = ((bf16[32,128,128]{2,1,0:T(8,128)(2,1)}), bf16[32,128,128]{2,1,0:T(8,128)(2,1)S(1)}, u32[]{:S(2)}, u32[]{:S(2)}) async-start(bf16[32,128,128]{2,1,0:T(8,128)(2,1)} %x_inverse.2), calls=%async_computation.3 | async-start | bytes 2097152 | tf_op jit(solution)/shard_map/all_to_all | solution.py:495
  74.6 2.9 %to_lanes.2.x_far = bf16[8192,128]{1,0:T(8,128)(2,1)S(1)} custom-call(bf16[128,64,128]{2,1,0:T(8,128)(2,1)} %bitcast.48), custom_call_target="tpu_custom_call" | custom-call | bytes 12582912 | tf_op jit(solution)/shard_map/to_lanes/pallas_call | solution.py:211
  77.5 1.3 copy-done.1
  78.8 0.1 broadcast_in_dim_tile.3.bias_ref
  78.9 0.1 copy.17
  79.0 0.1 reshape.114.mix_ref
  79.1 2.9 %to_lanes.3.cot_far = bf16[8192,128]{1,0:T(8,128)(2,1)S(1)} custom-call(bf16[128,64,128]{2,1,0:T(8,128)(2,1)} %bitcast.49), custom_call_target="tpu_custom_call" | custom-call | bytes 12582912 | tf_op jit(solution)/shard_map/to_lanes/pallas_call | solution.py:211
  82.0 1.3 copy-done.2
  83.3 18.9 %all-to-all-done.3.recv_ref = bf16[32,128,128]{2,1,0:T(8,128)(2,1)S(1)} async-done(((bf16[32,128,128]{2,1,0:T(8,128)(2,1)}), bf16[32,128,128]{2,1,0:T(8,128)(2,1)S(1)}, u32[]{:S(2)}, u32[]{:S(2)}) %all-to-all-start.3) | async-done | bytes 1048608 | tf_op jit(solution)/shard_map/all_to_all | solution.py:495
  102.2 5.8 %middle.1 = (bf16[32,128,128]{2,1,0:T(8,128)(2,1)S(1)}, bf16[8192,128]{1,0:T(8,128)(2,1)S(1)}, bf16[8192,128]{1,0:T(8,128)(2,1)S(1)}) custom-call(bf16[32,128,128]{2,1,0:T(8,128)(2,1)S(1)} %all-to-all-done.3.recv_ref, bf16[8192,128]{1,0:T(8,128)(2,1)} %copy-done.1, bf16[8192,128]{1,0:T(8,128)(2,1)} %copy-done.2, bf16[512,256]{1,0:T(8,128)(2,1)} %constant.77.clone.inv_far, ...), custom_call_target="tpu_custom_call" | custom-call | flops 1073741824 | bytes 12582912 | tf_op jit(solution)/shard_map/middle/pallas_call | solution.py:416
  108.1 32.2 %all_to_all.43.recv_ref = bf16[32,128,128]{2,1,0:T(8,128)(2,1)S(1)} all-to-all(bf16[32,128,128]{2,1,0:T(8,128)(2,1)S(1)} %get-tuple-element.37), channel_id=1, replica_groups=mesh['gz'=8,'xy'=32] {'xy'}, dimensions={0} | all-to-all | bytes 2097152 | tf_op jit(solution)/shard_map/all_to_all | solution.py:495
  140.3 0.3 x_forward.3
  140.6 10.0 %all_to_all.44.recv_ref = bf16[8,128,128]{2,1,0:T(8,128)(2,1)S(1)} all-to-all(bf16[8,128,128]{2,1,0:T(8,128)(2,1)S(1)} %x_forward.3), channel_id=1, replica_groups=mesh['gz'=8,'xy'=32] {'gz'}, dimensions={0} | all-to-all | bytes 524288 | tf_op jit(solution)/shard_map/all_to_all | solution.py:495
  150.7 0.3 z_forward.3
  151.0 0.1 reshape.116
  151.1 0.1 neg.3
  151.1 0.1 reshape.117
  151.2 0.4 maximum_bitcast_fusion
  151.6 1.2 fusion.11
  152.8 0.1 fusion.16
  152.9 0.1 reshape_squeeze.7.imag_ref
  153.0 0.1 reshape_squeeze.6.real_ref
  153.1 0.3 z_inverse.3
  153.4 9.9 %all_to_all.45.recv_ref = bf16[8,128,128]{2,1,0:T(8,128)(2,1)S(1)} all-to-all(bf16[8,128,128]{2,1,0:T(8,128)(2,1)S(1)} %z_inverse.3), channel_id=1, replica_groups=mesh['gz'=8,'xy'=32] {'gz'}, dimensions={0} | all-to-all | bytes 524288 | tf_op jit(solution)/shard_map/all_to_all | solution.py:495
  163.3 1.3 x_inverse.3
  164.6 5.6 %all-to-all-start.7 = ((bf16[32,128,128]{2,1,0:T(8,128)(2,1)}), bf16[32,128,128]{2,1,0:T(8,128)(2,1)S(1)}, u32[]{:S(2)}, u32[]{:S(2)}) async-start(bf16[32,128,128]{2,1,0:T(8,128)(2,1)} %x_inverse.3), calls=%async_computation.7 | async-start | bytes 2097152 | tf_op jit(solution)/shard_map/all_to_all | solution.py:495
  170.2 3.5 %from_lanes.1 = bf16[128,64,128]{2,1,0:T(8,128)(2,1)} custom-call(bf16[8192,128]{1,0:T(8,128)(2,1)} %copy-done.6), custom_call_target="tpu_custom_call" | custom-call | bytes 12582912 | tf_op jit(solution)/shard_map/from_lanes/pallas_call | solution.py:249
  173.8 2.2 %fusion.4 = bf16[1,4,32,64,128]{4,3,2,1,0:T(8,128)(2,1)} fusion(bf16[1,4,32,2,128]{4,3,0,2,1:T(2,128)(2,1)S(1)} %copy-done.13, bf16[1,4,32,2,128]{4,3,0,2,1:T(2,128)(2,1)S(1)} %get-tuple-element.45, bf16[1,4,32,2,64]{4,3,0,2,1:T(2,128)(2,1)S(1)} %bitcast.55, bf16[1,4,32,2,64]{4,3,0,2,1:T(2,128)(2,1)S(1)} %bitcast.53), kind=kOutput, calls=%fused_computation.5 | convolution fusion | flops 9830400 | bytes 2293760 | tf_op jit(solution)/shard_map/rkmbi,rkmbo->kmio/dot_general | solution.py:579
  176.0 21.9 %all-to-all-done.7.recv_ref = bf16[32,128,128]{2,1,0:T(8,128)(2,1)S(1)} async-done(((bf16[32,128,128]{2,1,0:T(8,128)(2,1)}), bf16[32,128,128]{2,1,0:T(8,128)(2,1)S(1)}, u32[]{:S(2)}, u32[]{:S(2)}) %all-to-all-start.7) | async-done | bytes 1048608 | tf_op jit(solution)/shard_map/all_to_all | solution.py:495
  197.9 3.9 %last.1 = bf16[128,64,128]{2,1,0:T(8,128)(2,1)} custom-call(bf16[32,128,128]{2,1,0:T(8,128)(2,1)S(1)} %all-to-all-done.7.recv_ref, bf16[8192,128]{1,0:T(8,128)(2,1)} %copy-done.5, bf16[256,512]{1,0:T(8,128)(2,1)S(1)} %copy-done.9, bf16[128,128]{1,0:T(8,128)(2,1)S(1)} %reshape.114.mix_ref), custom_call_target="tpu_custom_call" | custom-call | flops 1073741824 | bytes 8388608 | tf_op jit(solution)/shard_map/last/pallas_call | solution.py:476
  (37 shorter events, 0.1 us)
Async XLA Ops:
  0.6 55.6 %copy-start = (bf16[1,4,32,64,128]{4,3,2,1,0:T(8,128)(2,1)S(1)}, bf16[1,4,32,64,128]{4,3,2,1,0:T(8,128)(2,1)}, u32[]{:S(2)}) copy-start(bf16[1,4,32,64,128]{4,3,2,1,0:T(8,128)(2,1)} %param.18) | copy-start | bytes 6291460
  0.6 42.9 %copy-start.11 = (bf16[128,512]{1,0:T(8,128)(2,1)S(1)}, bf16[128,512]{1,0:T(8,128)(2,1)}, u32[]{:S(2)}) copy-start(bf16[128,512]{1,0:T(8,128)(2,1)} %constant.78.clone.table_ref) | copy-start | bytes 393220
  3.9 51.8 %copy-start.3 = (bf16[256,1024]{1,0:T(8,128)(2,1)S(1)}, bf16[256,1024]{1,0:T(8,128)(2,1)}, u32[]{:S(2)}) copy-start(bf16[256,1024]{1,0:T(8,128)(2,1)} %constant.80.clone.table_ref) | copy-start | bytes 1572868
  55.7 1.7 copy-start.7
  56.1 1.6 copy-start.14
  56.2 1.6 copy-start.16
  56.2 11.5 %copy-start.10 = (bf16[512,128]{1,0:T(8,128)(2,1)S(1)}, bf16[512,128]{1,0:T(8,128)(2,1)}, u32[]{:S(2)}) copy-start(bf16[512,128]{1,0:T(8,128)(2,1)} %constant.79.clone.table_ref) | copy-start | bytes 393220
  69.0 33.3 %all-to-all-start.3 = ((bf16[32,128,128]{2,1,0:T(8,128)(2,1)}), bf16[32,128,128]{2,1,0:T(8,128)(2,1)S(1)}, u32[]{:S(2)}, u32[]{:S(2)}) async-start(bf16[32,128,128]{2,1,0:T(8,128)(2,1)} %x_inverse.2), calls=%async_computation.3 | async-start | bytes 2097152 | tf_op jit(solution)/shard_map/all_to_all | solution.py:495
  74.5 4.3 %copy-start.19 = (f32[64]{0:T(128)S(1)}, f32[64]{0:T(128)}, u32[]{:S(2)}) copy-start(f32[64]{0:T(128)} %param.20) | copy-start | bytes 772
  74.6 4.3 %copy-start.18 = (bf16[64,64]{1,0:T(8,128)(2,1)S(1)}, bf16[64,64]{1,0:T(8,128)(2,1)}, u32[]{:S(2)}) copy-start(bf16[64,64]{1,0:T(8,128)(2,1)} %param.19) | copy-start | bytes 24580
  77.5 1.3 copy-start.1
  82.0 1.3 copy-start.2
  108.1 42.9 %copy-start.5 = (bf16[8192,128]{1,0:T(8,128)(2,1)}, bf16[8192,128]{1,0:T(8,128)(2,1)S(1)}, u32[]{:S(2)}) copy-start(bf16[8192,128]{1,0:T(8,128)(2,1)S(1)} %get-tuple-element.40.pre_ref) | copy-start | bytes 6291460
  108.1 42.9 %copy-start.6 = (bf16[8192,128]{1,0:T(8,128)(2,1)}, bf16[8192,128]{1,0:T(8,128)(2,1)S(1)}, u32[]{:S(2)}) copy-start(bf16[8192,128]{1,0:T(8,128)(2,1)S(1)} %get-tuple-element.36.x_ref) | copy-start | bytes 6291460
  108.1 42.6 %copy-start.4 = (bf16[256,1024]{1,0:T(8,128)(2,1)S(1)}, bf16[256,1024]{1,0:T(8,128)(2,1)}, u32[]{:S(2)}) copy-start(bf16[256,1024]{1,0:T(8,128)(2,1)} %constant.80.clone.table_ref) | copy-start | bytes 1572868
  150.7 2.4 %copy-start.8 = (bf16[1024,256]{1,0:T(8,128)(2,1)S(1)}, bf16[1024,256]{1,0:T(8,128)(2,1)}, u32[]{:S(2)}) copy-start(bf16[1024,256]{1,0:T(8,128)(2,1)} %constant.81.clone.table_ref) | copy-start | bytes 1572868
  151.6 11.7 %copy-start.12 = (bf16[1,4,32,2,128]{4,3,0,2,1:T(2,128)(2,1)}, bf16[1,4,32,2,128]{4,3,0,2,1:T(2,128)(2,1)S(1)}, u32[]{:S(2)}) copy-start(bf16[1,4,32,2,128]{4,3,0,2,1:T(2,128)(2,1)S(1)} %get-tuple-element.46) | copy-start | bytes 196612
  164.6 33.3 %all-to-all-start.7 = ((bf16[32,128,128]{2,1,0:T(8,128)(2,1)}), bf16[32,128,128]{2,1,0:T(8,128)(2,1)S(1)}, u32[]{:S(2)}, u32[]{:S(2)}) async-start(bf16[32,128,128]{2,1,0:T(8,128)(2,1)} %x_inverse.3), calls=%async_computation.7 | async-start | bytes 2097152 | tf_op jit(solution)/shard_map/all_to_all | solution.py:495
  170.2 3.6 %copy-start.13 = (bf16[1,4,32,2,128]{4,3,0,2,1:T(2,128)(2,1)S(1)}, bf16[1,4,32,2,128]{4,3,0,2,1:T(2,128)(2,1)}, u32[]{:S(2)}) copy-start(bf16[1,4,32,2,128]{4,3,0,2,1:T(2,128)(2,1)} %copy-done.12) | copy-start | bytes 196612
  170.2 3.6 %copy-start.15 = (bf16[1,4,32,2,64]{4,3,2,1,0:T(2,128)(2,1)S(1)}, bf16[1,4,32,2,64]{4,3,2,1,0:T(2,128)(2,1)}, u32[]{:S(2)}) copy-start(bf16[1,4,32,2,64]{4,3,2,1,0:T(2,128)(2,1)} %copy-done.14) | copy-start | bytes 98308
  170.2 3.6 %copy-start.17 = (bf16[1,4,32,2,64]{4,3,2,1,0:T(2,128)(2,1)S(1)}, bf16[1,4,32,2,64]{4,3,2,1,0:T(2,128)(2,1)}, u32[]{:S(2)}) copy-start(bf16[1,4,32,2,64]{4,3,2,1,0:T(2,128)(2,1)} %copy-done.16) | copy-start | bytes 98308
  173.8 24.1 %copy-start.9 = (bf16[256,512]{1,0:T(8,128)(2,1)S(1)}, bf16[256,512]{1,0:T(8,128)(2,1)}, u32[]{:S(2)}) copy-start(bf16[256,512]{1,0:T(8,128)(2,1)} %constant.75.clone.far_ref.inv_ref) | copy-start | bytes 786436
